TPU v7x, 32 devices: a whole 2x2x4 slice. The times are simulated.
32 devices in a mesh: sens: 8 (over y, x, core), hour: 4 (over z).
Axes of the slice: x: 2, y: 2, z: 4, core: 2. Of those that a mesh axis runs over, the one named last changes fastest.
Arguments:
- sky: bfloat16 [512, 146], P('hour'), may hold values from 0.049804688 to 1
- sky_open: bfloat16 [146, 16384], P(None, 'sens'), may hold values from 0 to 0.013977051
- sky_closed: bfloat16 [146, 16384], P(None, 'sens'), may hold values from 0 to 0.0039978027
- sun_coef: bfloat16 [5165, 16384], P(None, ('sens', 'hour')), may hold values from 0 to 1
- sun_bins: int32 [512, 4], P('hour'), may hold values from 0 to 5164, as said below
- sun_rad: bfloat16 [512, 4], P('hour'), may hold values from 0.099609375 to 1
- target: bfloat16 [512, 16384], P('hour', 'sens'), may hold values from 0 to 2
- zone_of: int32 [8192, 1], P('sens'), may hold values from 0 to 7
- area: float32 [8192], P('sens'), may hold values from 0.5 to 4
- openness: float32 [8192], P('sens'), may hold values from 0 to 1
Outputs:
- illuminance: bfloat16 [512, 16384], P('hour', 'sens')
- new_openness: float32 [8192], P('sens')
Inputs may be any that keep to these rules, and one draw needn't show every extreme that they name: `sun_bins`: the 4 bins of one hour are consecutive modulo 5165, hence distinct. `zone_of`: every zone has at least one window.
All inputs are finite; a program needn't handle non-finite values.
Results may differ from a plain program's by a relative error of at most 0.001.
Values may be sent and summed in bfloat16 or wider, within the bound.
No kernel may reach another device: no remote copies, remote signals or barrier semaphores. Data moves between devices by JAX's collectives and lax.ppermute only.
A program may use at most 128 MiB of HBM per device.

v0:
```python
import jax
import jax.numpy as jnp
from jax import lax
from jax.experimental import pallas as pl
from jax.experimental.pallas import tpu as pltpu
from jax.sharding import PartitionSpec as P

LANES = 128
CHUNK = 8
HEAD = 16
TAIL = 8
FRONT = 2
PATTERN = jnp.bfloat16
LEVELS = 65000.0
VMEM_BYTES = 40 * 1024 * 1024
ANY = pl.BlockSpec(memory_space=pl.ANY)
HBM = pl.BlockSpec(memory_space=pltpu.HBM)
SMEM = pl.BlockSpec(memory_space=pltpu.SMEM)
VMEM = pl.BlockSpec(memory_space=pltpu.VMEM)


def call(kernel, name, out_shape, flops=0, moved=0, **more):
    run = pl.pallas_call(
        kernel,
        out_shape=out_shape,
        name=name,
        compiler_params=pltpu.CompilerParams(vmem_limit_bytes=VMEM_BYTES),
        cost_estimate=pl.CostEstimate(flops=flops, bytes_accessed=moved, transcendentals=0),
        **more,
    )
    specs = more["in_specs"]
    return lambda *args: run(
        *[pltpu.with_memory_space_constraint(x, pltpu.HBM) if s is HBM else x for x, s in zip(args, specs)]
    )


def exchange(x, axis, mask):
    return lax.ppermute(x, axis, [(i, i ^ mask) for i in range(lax.axis_size(axis))])


def fetch(pairs, sems):
    copies = [pltpu.make_async_copy(source, place, sems.at[i]) for i, (source, place) in enumerate(pairs)]
    for c in copies:
        c.start()
    return copies


def pack_kernel(bins_hbm, rad_hbm, out_ref, bins_ref, rad_ref, sems):
    for c in fetch([(bins_hbm, bins_ref), (rad_hbm, rad_ref)], sems):
        c.wait()
    bins = bins_ref[:]
    kbins = bins.shape[0]
    fill = jnp.zeros((HEAD - 3 * kbins, bins.shape[1]), jnp.float32)
    parts = [rad_ref[:].astype(jnp.float32), (bins // LANES).astype(jnp.float32), (bins % LANES).astype(jnp.float32)]
    out_ref[:] = jnp.concatenate(parts + [fill], axis=0).astype(jnp.bfloat16)


def sums_kernel(zones):
    def kernel(zone_hbm, area_hbm, openness_hbm, sums_ref, zone_ref, area_ref, openness_ref, sems):
        for c in fetch([(zone_hbm, zone_ref), (area_hbm, area_ref), (openness_hbm, openness_ref)], sems):
            c.wait()
        zone, area = zone_ref[:], area_ref[:]
        lane = lax.broadcasted_iota(jnp.int32, sums_ref.shape, 1)
        values = [area * openness_ref[:], area, area * area]
        row = jnp.zeros(sums_ref.shape, jnp.float32)
        for z in range(zones):
            member = zone == z
            for k, value in enumerate(values):
                total = jnp.sum(jnp.where(member, value, 0.0), keepdims=True)
                row = jnp.where(lane == FRONT + 3 * z + k, total, row)
        sums_ref[:] = row

    return kernel


def sun_kernel(count, kbins, stream):
    def kernel(coef_in, *refs):
        heads, outs, rest = refs[:count], refs[count : 2 * count], refs[2 * count :]
        rows = heads[0].shape[1]
        nbins = coef_in.shape[0]
        step = CHUNK * LANES
        spans = [(first, min(first + step, nbins)) for first in range(0, nbins, step)]
        if stream:
            coef_ref, acc, pattern, block, sems = rest
            cuts = spans[:-2] + [(spans[-2][0], nbins)]
            at = [pl.ds(first, end - first) for first, end in cuts]
            copies = fetch([(coef_in.at[a], coef_ref.at[a]) for a in at], sems)
        else:
            coef_ref, (acc, pattern, block) = coef_in, rest
        lane = lax.broadcasted_iota(jnp.int32, (rows, LANES), 1)
        for g in range(count):
            small = heads[g][:].astype(jnp.float32).T
            value = jnp.zeros((rows, LANES), jnp.float32)
            where = jnp.zeros((rows, LANES), jnp.float32)
            for k in range(kbins):
                low = small[:, 2 * kbins + k : 2 * kbins + k + 1].astype(jnp.int32)
                hit = lane == low
                value = jnp.where(hit, small[:, k : k + 1], value)
                where = jnp.where(hit, small[:, kbins + k : kbins + k + 1], where)
            pattern[g * rows : (g + 1) * rows] = value.astype(pattern.dtype)
            block[g * rows : (g + 1) * rows] = where.astype(block.dtype)

        for i, (first, end) in enumerate(spans):
            parts = []
            for c in range(first // LANES, pl.cdiv(end, LANES)):
                here = block[:] == jnp.asarray(c, block.dtype)
                parts.append(jnp.where(here, pattern[:], jnp.zeros_like(pattern)).astype(jnp.bfloat16))
            weights = jnp.concatenate(parts, axis=1) if len(parts) > 1 else parts[0]
            if stream and i < len(copies):
                copies[i].wait()
            part = jnp.dot(weights[:, : end - first], coef_ref[first:end], preferred_element_type=jnp.float32)
            acc[:] = part if first == 0 else acc[:] + part

        for g in range(count):
            sun = acc[g * rows : (g + 1) * rows]
            power = jnp.ceil(jnp.log2(jnp.maximum(jnp.max(sun, axis=0, keepdims=True), 1e-30)))
            code = jnp.round(sun * (LEVELS / jnp.exp2(power)) - 0.5 * LEVELS)
            outs[g][:rows] = code.astype(jnp.int32).astype(jnp.int16)
            power = jnp.broadcast_to(power, (TAIL, power.shape[1]))
            outs[g][rows:] = power.astype(jnp.int32).astype(jnp.int16)

    return kernel


def base_kernel(
    token, sky_hbm, open_hbm, closed_hbm, target_hbm, cross_ref, closed_out, target_out, sky_ref, open_ref, closed_ref, sems
):
    pairs = [(sky_hbm, sky_ref), (open_hbm, open_ref), (closed_hbm, closed_ref), (target_hbm, target_out)]
    copies = fetch(pairs, sems)
    for c in copies[:3]:
        c.wait()
    over = (((0,), (0,)), ((), ()))
    closed = lax.dot_general(sky_ref[:], closed_ref[:], over, preferred_element_type=jnp.float32)
    opened = lax.dot_general(sky_ref[:], open_ref[:], over, preferred_element_type=jnp.float32)
    closed_out[:] = closed
    cross_ref[:] = opened - closed
    copies[3].wait()


def place(me_ref, mask, width):
    return pl.ds(pl.multiple_of((me_ref[0] ^ mask) * width, LANES), width)


def cross_of(codes, base):
    rows = base.shape[0]
    scale = jnp.exp2(codes[rows:].astype(jnp.int32).astype(jnp.float32)[:1]) / LEVELS
    sun = (codes[:rows].astype(jnp.int32).astype(jnp.float32) + 0.5 * LEVELS) * scale
    return base + sun


def grad_terms(me_ref, base_ref, closed_ref, target_ref, codes, masks, linear, square):
    rows, width = base_ref.shape[0], codes[0].shape[1]
    for mask, code in zip(masks, codes):
        at = place(me_ref, mask, width)
        cross = cross_of(code, base_ref[:, at])
        apart = closed_ref[:, at] - target_ref[:, at].astype(jnp.float32)
        linear = linear + jnp.sum((apart * cross).reshape(rows // 8, 8, width), axis=0)
        square = square + jnp.sum((cross * cross).reshape(rows // 8, 8, width), axis=0)
    return linear, square


def near_kernel(masks):
    def kernel(me_ref, base_ref, closed_ref, target_ref, *refs):
        codes, out_ref = refs[:-1], refs[-1]
        zero = jnp.zeros(out_ref.shape[1:], jnp.float32)
        out_ref[0], out_ref[1] = grad_terms(me_ref, base_ref, closed_ref, target_ref, codes, masks, zero, zero)

    return kernel


def far_kernel(masks):
    def kernel(me_ref, base_ref, closed_ref, target_ref, near_ref, sums_ref, *refs):
        codes, out_ref = refs[:-1], refs[-1]
        linear, square = grad_terms(
            me_ref, base_ref, closed_ref, target_ref, codes, masks, near_ref[0], near_ref[1]
        )
        lane = lax.broadcasted_iota(jnp.int32, sums_ref.shape, 1)
        row = jnp.where(lane == 0, 2.0 * jnp.sum(linear, keepdims=True), sums_ref[:])
        row = jnp.where(lane == 1, 2.0 * jnp.sum(square, keepdims=True), row)
        out_ref[:] = jnp.broadcast_to(row[None], out_ref.shape)

    return kernel


def last_kernel(groups, zones, windows):
    def kernel(place_ref, own_ref, heard_ref, zone_ref, area_ref, openness_ref, base_ref, closed_ref, *refs):
        codes, (lit_ref, step_ref) = refs[:groups], refs[groups:]
        sums = heard_ref[0]
        for z in range(1, zones):
            sums = sums + heard_ref[z * groups]
        zone = zone_ref[:]
        chosen = jnp.zeros(zone.shape, jnp.float32)
        square = jnp.zeros((1, 1), jnp.float32)
        own_share = jnp.zeros((1, 1), jnp.float32)
        for z in range(zones):
            at = FRONT + 3 * z
            num, den, squares = sums[:, at : at + 1], sums[:, at + 1 : at + 2], sums[:, at + 2 : at + 3]
            share = num / den
            both = jnp.sum(heard_ref[z * groups : (z + 1) * groups], axis=0)
            ratio = (both[:, 0:1] + share * both[:, 1:2]) / den
            square = square + ratio * ratio * squares
            chosen = jnp.where(zone == z, ratio, chosen)
            own_share = jnp.where(own_ref[0] == z, share, own_share)
        rms = jnp.sqrt(square / windows + 1e-06)
        step_ref[:] = jnp.clip(openness_ref[:] - 0.25 * (area_ref[:] * chosen) / rms, 0.0, 1.0)
        width = codes[0].shape[1]
        for mask in range(groups):
            at = place(place_ref, mask, width)
            lit = closed_ref[:, at] + own_share * cross_of(codes[mask], base_ref[:, at])
            lit_ref[:, at] = lit.astype(jnp.bfloat16)

    return kernel


def local(sky, sky_open, sky_closed, sun_coef, sun_bins, sun_rad, target, zone_of, area, openness):
    zones = lax.axis_size("sens")
    groups = lax.axis_size("hour")
    me = lax.axis_index("hour").astype(jnp.int32)[None]
    own_zone = lax.axis_index("sens").astype(jnp.int32)[None]
    rows, patches = sky.shape
    kbins = sun_bins.shape[1]
    nbins, width = sun_coef.shape
    hours = rows * groups
    sensors = groups * width
    windows = area.shape[0]
    assert nbins % LANES == 0 or nbins % LANES >= 2 * kbins
    assert nbins <= 256 * LANES and width % LANES == 0 and windows % LANES == 0 and 3 * kbins <= HEAD
    assert groups & (groups - 1) == 0 and groups > 1 and rows % 16 == 0
    shape = jax.ShapeDtypeStruct
    f32, bf16 = jnp.float32, jnp.bfloat16
    dma = lambda n: pltpu.SemaphoreType.DMA((n,))

    packed = call(
        pack_kernel,
        "pack",
        shape((HEAD, rows), bf16),
        in_specs=[HBM, HBM],
        scratch_shapes=[pltpu.VMEM((kbins, rows), jnp.int32), pltpu.VMEM((kbins, rows), bf16), dma(2)],
    )(sun_bins.T, sun_rad.T)
    order = list(range(groups))[::-1]
    heads = {mask: exchange(packed, "hour", mask) if mask else packed for mask in order}

    tiles = (windows // LANES, LANES)
    message = pl.cdiv(FRONT + 3 * zones, LANES) * LANES
    zone_sums, zone2, area2, openness2 = call(
        sums_kernel(zones),
        "sums",
        [shape((1, message), f32), shape(tiles, jnp.int32), shape(tiles, f32), shape(tiles, f32)],
        in_specs=[HBM] * 3,
        out_specs=[VMEM] * 4,
        scratch_shapes=[dma(3)],
    )(zone_of.reshape(tiles), area.reshape(tiles), openness.reshape(tiles))

    def sun(masks, coef, stream):
        count = len(masks)
        outs = [shape((rows + TAIL, width), jnp.int16)] * count
        scratch = [pltpu.VMEM((count * rows, width), f32)] + [pltpu.VMEM((count * rows, LANES), PATTERN)] * 2
        found = call(
            sun_kernel(count, kbins, stream),
            "sun",
            outs + [shape((nbins, width), bf16)] * stream,
            flops=2 * count * rows * nbins * width * stream,
            moved=2 * nbins * width * stream,
            in_specs=[HBM if stream else VMEM] + [VMEM] * count,
            out_specs=[VMEM] * (count + stream),
            scratch_shapes=scratch + [dma(pl.cdiv(nbins, CHUNK * LANES))] * stream,
        )(coef, *[heads[mask] for mask in masks])
        return dict(zip(masks, found)), found[-1]

    assert nbins > CHUNK * LANES
    far, near = order[: groups // 2], order[groups // 2 :]
    suns, coef = sun(far, sun_coef, 1)
    codes = {mask: exchange(x, "hour", mask) for mask, x in suns.items()}
    suns, _ = sun(near, coef, 0)
    codes |= {mask: exchange(x, "hour", mask) if mask else x for mask, x in suns.items()}

    base, closed, wanted = call(
        base_kernel,
        "base",
        [shape((rows, sensors), f32)] * 2 + [shape((rows, sensors), bf16)],
        in_specs=[ANY] + [HBM] * 4,
        out_specs=[VMEM] * 3,
        scratch_shapes=[
            pltpu.VMEM((patches, rows), bf16),
            pltpu.VMEM((patches, sensors), bf16),
            pltpu.VMEM((patches, sensors), bf16),
            dma(4),
        ],
    )(codes[0], sky.T, sky_open, sky_closed, target)
    near_sums = call(
        near_kernel(near),
        "near",
        shape((2, 8, width), f32),
        in_specs=[SMEM] + [VMEM] * (3 + len(near)),
    )(me, base, closed, wanted, *[codes[mask] for mask in near])
    sent = call(
        far_kernel(far),
        "far",
        shape((zones * groups, 1, message), f32),
        in_specs=[SMEM] + [VMEM] * (5 + len(far)),
    )(me, base, closed, wanted, near_sums, zone_sums, *[codes[mask] for mask in far])
    heard = lax.all_to_all(sent, ("sens", "hour"), 0, 0)
    illuminance, new_openness = call(
        last_kernel(groups, zones, windows * zones),
        "last",
        [shape((rows, sensors), bf16), shape(tiles, f32)],
        in_specs=[SMEM] * 2 + [VMEM] * (6 + groups),
    )(me, own_zone, heard, zone2, area2, openness2, base, closed, *[codes[mask] for mask in range(groups)])
    return (illuminance, new_openness.reshape(-1))


def solution(mesh):
    in_specs = (
        P("hour", None),
        P(None, "sens"),
        P(None, "sens"),
        P(None, ("sens", "hour")),
        P("hour", None),
        P("hour", None),
        P("hour", "sens"),
        P("sens", None),
        P("sens"),
        P("sens"),
    )
    out_specs = (P("hour", "sens"), P("sens"))
    return jax.shard_map(local, mesh=mesh, in_specs=in_specs, out_specs=out_specs, check_vma=False)
```

profile of v0, /device:TPU:0, one launch (start us, length us, event | category | flops | bytes accessed | tf_op | source)
XLA Modules:
  0.0 44.7 jit_solution(1530968012239811537)
XLA Ops:
  0.6 0.7 %pack.1.refs_1_ = bf16[16,128]{1,0:T(8,128)(2,1)S(1)} custom-call(s32[4,128]{1,0:T(4,128)} %bitcast.13, bf16[4,128]{1,0:T(4,128)(2,1)} %bitcast.14), custom_call_target="tpu_custom_call" | custom-call | tf_op jit(solution)/shard_map/pack/pallas_call | solution.py:32
  1.4 5.1 %collective-permute-start = (bf16[16,128]{1,0:T(8,128)(2,1)S(1)}, bf16[16,128]{1,0:T(8,128)(2,1)S(1)}, u32[]{:S(2)}, u32[]{:S(2)}) collective-permute-start(bf16[16,128]{1,0:T(8,128)(2,1)S(1)} %pack.1.refs_1_), channel_id=1, source_target_pairs={{0,3},{1,2},{2,1},{3,0},{4,7},{5,6},{6,5},{7,4},{8,11},{9,10},{10,... | collective-permute-start | bytes 12296 | tf_op jit(solution)/shard_map/ppermute | solution.py:38
  6.5 0.0 collective-permute-start.1
  6.5 0.6 %collective-permute-start.2 = (bf16[16,128]{1,0:T(8,128)(2,1)S(1)}, bf16[16,128]{1,0:T(8,128)(2,1)S(1)}, u32[]{:S(2)}, u32[]{:S(2)}) collective-permute-start(bf16[16,128]{1,0:T(8,128)(2,1)S(1)} %pack.1.refs_1_), channel_id=1, source_target_pairs={{0,1},{1,0},{2,3},{3,2},{4,5},{5,4},{6,7},{7,6},{8,9},{9,8},{10,11... | collective-permute-start | bytes 12296 | tf_op jit(solution)/shard_map/ppermute | solution.py:38
  7.1 0.9 %collective-permute-done.refs_0_ = bf16[16,128]{1,0:T(8,128)(2,1)S(1)} collective-permute-done((bf16[16,128]{1,0:T(8,128)(2,1)S(1)}, bf16[16,128]{1,0:T(8,128)(2,1)S(1)}, u32[]{:S(2)}, u32[]{:S(2)}) %collective-permute-start) | collective-permute-done | bytes 4128 | tf_op jit(solution)/shard_map/ppermute | solution.py:38
  8.1 2.9 %collective-permute-done.1.refs_1_ = bf16[16,128]{1,0:T(8,128)(2,1)S(1)} collective-permute-done((bf16[16,128]{1,0:T(8,128)(2,1)S(1)}, bf16[16,128]{1,0:T(8,128)(2,1)S(1)}, u32[]{:S(2)}, u32[]{:S(2)}) %collective-permute-start.1) | collective-permute-done | bytes 4128 | tf_op jit(solution)/shard_map/ppermute | solution.py:38
  11.0 4.0 %sun.2 = (s16[136,512]{1,0:T(8,128)(2,1)S(1)}, s16[136,512]{1,0:T(8,128)(2,1)S(1)}, bf16[5165,512]{1,0:T(8,128)(2,1)S(1)}) custom-call(bf16[5165,512]{1,0:T(8,128)(2,1)} %coef_in.1, bf16[16,128]{1,0:T(8,128)(2,1)S(1)} %collective-permute-done.refs_0_, bf16[16,128]{1,0:T(8,128)(2,1)S(1)} %collective-permute-done.1.refs_1_), custom_call_target="tpu_custom_call" | custom-call | flops 1353973760 | bytes 5288960 | tf_op jit(solution)/shard_map/sun/pallas_call | solution.py:32
  15.0 0.0 collective-permute-done.2.refs_0_
  15.0 2.2 %sun.3 = (s16[136,512]{1,0:T(8,128)(2,1)S(1)}, s16[136,512]{1,0:T(8,128)(2,1)S(1)}) custom-call(bf16[5165,512]{1,0:T(8,128)(2,1)S(1)} %get-tuple-element.16.coef_in, bf16[16,128]{1,0:T(8,128)(2,1)S(1)} %collective-permute-done.2.refs_0_, bf16[16,128]{1,0:T(8,128)(2,1)S(1)} %pack.1.refs_1_), custom_call_target="tpu_custom_call" | custom-call | tf_op jit(solution)/shard_map/sun/pallas_call | solution.py:32
  17.2 0.1 collective-permute-start.3
  17.3 1.5 %collective-permute-start.4 = (s16[136,512]{1,0:T(8,128)(2,1)S(1)}, s16[136,512]{1,0:T(8,128)(2,1)S(1)}, u32[]{:S(2)}, u32[]{:S(2)}) collective-permute-start(s16[136,512]{1,0:T(8,128)(2,1)S(1)} %get-tuple-element.23), channel_id=1, source_target_pairs={{0,3},{1,2},{2,1},{3,0},{4,7},{5,6},{6,5},{7,4},{8,11},{9,10},{10,... | collective-permute-start | bytes 417800 | tf_op jit(solution)/shard_map/ppermute | solution.py:38
  18.8 2.0 %collective-permute-start.5 = (s16[136,512]{1,0:T(8,128)(2,1)S(1)}, s16[136,512]{1,0:T(8,128)(2,1)S(1)}, u32[]{:S(2)}, u32[]{:S(2)}) collective-permute-start(s16[136,512]{1,0:T(8,128)(2,1)S(1)} %get-tuple-element.24), channel_id=1, source_target_pairs={{0,2},{1,3},{2,0},{3,1},{4,6},{5,7},{6,4},{7,5},{8,10},{9,11},{10,... | collective-permute-start | bytes 417800 | tf_op jit(solution)/shard_map/ppermute | solution.py:38
  20.8 0.9 %sums.1 = (f32[1,128]{1,0:T(1,128)S(1)}, s32[8,128]{1,0:T(8,128)S(1)}, f32[8,128]{1,0:T(8,128)S(1)}, f32[8,128]{1,0:T(8,128)S(1)}) custom-call(s32[8,128]{1,0:T(8,128)} %bitcast.10, f32[8,128]{1,0:T(8,128)} %bitcast.11, f32[8,128]{1,0:T(8,128)} %bitcast.12), custom_call_target="tpu_custom_call" | custom-call | tf_op jit(solution)/shard_map/sums/pallas_call | solution.py:32
  21.7 1.8 %base.1 = (f32[128,2048]{1,0:T(8,128)S(1)}, f32[128,2048]{1,0:T(8,128)S(1)}, bf16[128,2048]{1,0:T(8,128)(2,1)S(1)}) custom-call(s16[136,512]{1,0:T(8,128)(2,1)S(1)} %get-tuple-element.17.token.refs_1_.refs_0_, bf16[146,128]{1,0:T(8,128)(2,1)} %bitcast.9, bf16[146,2048]{1,0:T(8,128)(2,1)} %open_hbm.1, bf16[146,2048]{1,0:T(8,128)(2,1)} %closed_hbm.1, ...), custom_call_target="tpu_custom_call" | custom-call | tf_op jit(solution)/shard_map/base/pallas_call | solution.py:32
  23.4 1.0 %collective-permute-done.3.refs_0_.refs_1_ = s16[136,512]{1,0:T(8,128)(2,1)S(1)} collective-permute-done((s16[136,512]{1,0:T(8,128)(2,1)S(1)}, s16[136,512]{1,0:T(8,128)(2,1)S(1)}, u32[]{:S(2)}, u32[]{:S(2)}) %collective-permute-start.3) | collective-permute-done | bytes 139296 | tf_op jit(solution)/shard_map/ppermute | solution.py:38
  24.4 0.2 near.1.near_ref
  24.7 1.4 %collective-permute-done.4.refs_0_.refs_3_ = s16[136,512]{1,0:T(8,128)(2,1)S(1)} collective-permute-done((s16[136,512]{1,0:T(8,128)(2,1)S(1)}, s16[136,512]{1,0:T(8,128)(2,1)S(1)}, u32[]{:S(2)}, u32[]{:S(2)}) %collective-permute-start.4) | collective-permute-done | bytes 139296 | tf_op jit(solution)/shard_map/ppermute | solution.py:38
  26.1 5.3 %collective-permute-done.5.refs_1_.refs_2_ = s16[136,512]{1,0:T(8,128)(2,1)S(1)} collective-permute-done((s16[136,512]{1,0:T(8,128)(2,1)S(1)}, s16[136,512]{1,0:T(8,128)(2,1)S(1)}, u32[]{:S(2)}, u32[]{:S(2)}) %collective-permute-start.5) | collective-permute-done | bytes 139296 | tf_op jit(solution)/shard_map/ppermute | solution.py:38
  31.4 1.0 %far.1 = f32[32,1,128]{2,1,0:T(1,128)} custom-call(s32[1]{0:T(128)} %bitcast.me_ref.place_ref, f32[128,2048]{1,0:T(8,128)S(1)} %get-tuple-element.18.base_ref, f32[128,2048]{1,0:T(8,128)S(1)} %get-tuple-element.19.closed_ref, bf16[128,2048]{1,0:T(8,128)(2,1)S(1)} %get-tuple-element.20.target_ref, f32[2,8,512]{2,1,0:T(8,128)S(1)} %near.1.near_ref, ...), custom_call_target="tpu_custom_call" | custom-call | tf_op jit(solution)/shard_map/far/pallas_call | solution.py:32
  32.4 3.4 %all-to-all-start = ((f32[32,1,128]{2,1,0:T(1,128)}), f32[32,1,128]{2,1,0:T(1,128)S(1)}, u32[]{:S(2)}, u32[]{:S(2)}) async-start(f32[32,1,128]{2,1,0:T(1,128)} %far.1), calls=%async_computation | async-start | bytes 32768 | tf_op jit(solution)/shard_map/all_to_all | solution.py:302
  35.8 7.1 %all-to-all-done.heard_ref = f32[32,1,128]{2,1,0:T(1,128)S(1)} async-done(((f32[32,1,128]{2,1,0:T(1,128)}), f32[32,1,128]{2,1,0:T(1,128)S(1)}, u32[]{:S(2)}, u32[]{:S(2)}) %all-to-all-start) | async-done | bytes 16416 | tf_op jit(solution)/shard_map/all_to_all | solution.py:302
  42.9 1.7 %last.1 = (bf16[128,2048]{1,0:T(8,128)(2,1)}, f32[8,128]{1,0:T(8,128)}) custom-call(s32[1]{0:T(128)} %bitcast.me_ref.place_ref, s32[1]{0:T(128)} %bitcast.1.own_ref, f32[32,1,128]{2,1,0:T(1,128)S(1)} %all-to-all-done.heard_ref, s32[8,128]{1,0:T(8,128)S(1)} %get-tuple-element.25.zone_ref, f32[8,128]{1,0:T(8,128)S(1)} %get-tuple-element.26.area_ref, ...), custom_call_target="tpu_custom_call" | custom-call | tf_op jit(solution)/shard_map/last/pallas_call | solution.py:32
Async XLA Ops:
  1.4 6.7 %collective-permute-start = (bf16[16,128]{1,0:T(8,128)(2,1)S(1)}, bf16[16,128]{1,0:T(8,128)(2,1)S(1)}, u32[]{:S(2)}, u32[]{:S(2)}) collective-permute-start(bf16[16,128]{1,0:T(8,128)(2,1)S(1)} %pack.1.refs_1_), channel_id=1, source_target_pairs={{0,3},{1,2},{2,1},{3,0},{4,7},{5,6},{6,5},{7,4},{8,11},{9,10},{10,... | collective-permute-start | bytes 12296 | tf_op jit(solution)/shard_map/ppermute | solution.py:38
  6.5 4.5 %collective-permute-start.1 = (bf16[16,128]{1,0:T(8,128)(2,1)S(1)}, bf16[16,128]{1,0:T(8,128)(2,1)S(1)}, u32[]{:S(2)}, u32[]{:S(2)}) collective-permute-start(bf16[16,128]{1,0:T(8,128)(2,1)S(1)} %pack.1.refs_1_), channel_id=1, source_target_pairs={{0,2},{1,3},{2,0},{3,1},{4,6},{5,7},{6,4},{7,5},{8,10},{9,11},{10,... | collective-permute-start | bytes 12296 | tf_op jit(solution)/shard_map/ppermute | solution.py:38
  6.5 8.5 %collective-permute-start.2 = (bf16[16,128]{1,0:T(8,128)(2,1)S(1)}, bf16[16,128]{1,0:T(8,128)(2,1)S(1)}, u32[]{:S(2)}, u32[]{:S(2)}) collective-permute-start(bf16[16,128]{1,0:T(8,128)(2,1)S(1)} %pack.1.refs_1_), channel_id=1, source_target_pairs={{0,1},{1,0},{2,3},{3,2},{4,5},{5,4},{6,7},{7,6},{8,9},{9,8},{10,11... | collective-permute-start | bytes 12296 | tf_op jit(solution)/shard_map/ppermute | solution.py:38
  17.2 7.2 %collective-permute-start.3 = (s16[136,512]{1,0:T(8,128)(2,1)S(1)}, s16[136,512]{1,0:T(8,128)(2,1)S(1)}, u32[]{:S(2)}, u32[]{:S(2)}) collective-permute-start(s16[136,512]{1,0:T(8,128)(2,1)S(1)} %get-tuple-element.21), channel_id=1, source_target_pairs={{0,1},{1,0},{2,3},{3,2},{4,5},{5,4},{6,7},{7,6},{8,9},{9,8},{10,11... | collective-permute-start | bytes 417800 | tf_op jit(solution)/shard_map/ppermute | solution.py:38
  17.3 8.8 %collective-permute-start.4 = (s16[136,512]{1,0:T(8,128)(2,1)S(1)}, s16[136,512]{1,0:T(8,128)(2,1)S(1)}, u32[]{:S(2)}, u32[]{:S(2)}) collective-permute-start(s16[136,512]{1,0:T(8,128)(2,1)S(1)} %get-tuple-element.23), channel_id=1, source_target_pairs={{0,3},{1,2},{2,1},{3,0},{4,7},{5,6},{6,5},{7,4},{8,11},{9,10},{10,... | collective-permute-start | bytes 417800 | tf_op jit(solution)/shard_map/ppermute | solution.py:38
  18.8 12.6 %collective-permute-start.5 = (s16[136,512]{1,0:T(8,128)(2,1)S(1)}, s16[136,512]{1,0:T(8,128)(2,1)S(1)}, u32[]{:S(2)}, u32[]{:S(2)}) collective-permute-start(s16[136,512]{1,0:T(8,128)(2,1)S(1)} %get-tuple-element.24), channel_id=1, source_target_pairs={{0,2},{1,3},{2,0},{3,1},{4,6},{5,7},{6,4},{7,5},{8,10},{9,11},{10,... | collective-permute-start | bytes 417800 | tf_op jit(solution)/shard_map/ppermute | solution.py:38
  32.4 10.5 %all-to-all-start = ((f32[32,1,128]{2,1,0:T(1,128)}), f32[32,1,128]{2,1,0:T(1,128)S(1)}, u32[]{:S(2)}, u32[]{:S(2)}) async-start(f32[32,1,128]{2,1,0:T(1,128)} %far.1), calls=%async_computation | async-start | bytes 32768 | tf_op jit(solution)/shard_map/all_to_all | solution.py:302
where the time goes:
time: 45 us; the launch traced here: 44.7 us
  waiting for transfers between devices  18.7 us (42%)
  starting transfers between devices  12.7 us (28%)
  Pallas kernels  12.6 us (28%)
  between operations  0.7 us (2%)
    pallas_call x8, Pallas kernels, call(): run(*[pltpu.with_memory_space_constraint(x, pltpu.HBM) if s is HBM else x...  12.6 us
    ppermute x6, waiting for transfers between devices, exchange(): lax.ppermute(x, axis, [(i, i ^ mask) for i in range(lax.axis_size(axis))])  11.6 us
    ppermute x6, starting transfers between devices, exchange(): lax.ppermute(x, axis, [(i, i ^ mask) for i in range(lax.axis_size(axis))])  9.3 us
    all_to_all x1, waiting for transfers between devices, local(): heard = lax.all_to_all(sent, ('sens', 'hour'), 0, 0)  7.09 us
    all_to_all x1, starting transfers between devices, local(): heard = lax.all_to_all(sent, ('sens', 'hour'), 0, 0)  3.44 us
  transfers between devices with their start and end apart: 7, of which 6 were waited for; matrix products, arithmetic and copies ran while one was open for 0% of the time, Pallas kernels for 15%

commit v1 on v0

--- a/solution.py
+++ b/solution.py
@@ -9,7 +9,6 @@
 CHUNK = 8
 HEAD = 16
 TAIL = 8
-FRONT = 2
 PATTERN = jnp.bfloat16
 LEVELS = 65000.0
 VMEM_BYTES = 40 * 1024 * 1024
@@ -55,9 +54,11 @@
     out_ref[:] = jnp.concatenate(parts + [fill], axis=0).astype(jnp.bfloat16)
 
 
-def sums_kernel(zones):
-    def kernel(zone_hbm, area_hbm, openness_hbm, sums_ref, zone_ref, area_ref, openness_ref, sems):
-        for c in fetch([(zone_hbm, zone_ref), (area_hbm, area_ref), (openness_hbm, openness_ref)], sems):
+def fetch_kernel(zones):
+    def kernel(coef_hbm, zone_hbm, area_hbm, openness_hbm, coef_ref, sums_ref, zone_ref, area_ref, openness_ref, sems):
+        pairs = [(zone_hbm, zone_ref), (area_hbm, area_ref), (openness_hbm, openness_ref)]
+        copies = fetch(pairs + [(coef_hbm.at[pl.ds(0, coef_ref.shape[0])], coef_ref)], sems)
+        for c in copies[:3]:
             c.wait()
         zone, area = zone_ref[:], area_ref[:]
         lane = lax.broadcasted_iota(jnp.int32, sums_ref.shape, 1)
@@ -67,29 +68,45 @@
             member = zone == z
             for k, value in enumerate(values):
                 total = jnp.sum(jnp.where(member, value, 0.0), keepdims=True)
-                row = jnp.where(lane == FRONT + 3 * z + k, total, row)
+                row = jnp.where(lane == (2 + k) * zones + z, total, row)
         sums_ref[:] = row
-
-    return kernel
-
-
-def sun_kernel(count, kbins, stream):
-    def kernel(coef_in, *refs):
-        heads, outs, rest = refs[:count], refs[count : 2 * count], refs[2 * count :]
+        copies[3].wait()
+
+    return kernel
+
+
+def sun_kernel(sources, kbins, stream):
+    count = len(sources)
+    inputs = 1 + max(operand for operand, _ in sources)
+
+    def kernel(first_ref, rest_in, *refs):
+        heads, outs, rest = refs[:inputs], refs[inputs : inputs + count], refs[inputs + count :]
         rows = heads[0].shape[1]
-        nbins = coef_in.shape[0]
+        split = first_ref.shape[0]
+        nbins = split + rest_in.shape[0] - (split if stream else 0)
         step = CHUNK * LANES
         spans = [(first, min(first + step, nbins)) for first in range(0, nbins, step)]
         if stream:
-            coef_ref, acc, pattern, block, sems = rest
-            cuts = spans[:-2] + [(spans[-2][0], nbins)]
-            at = [pl.ds(first, end - first) for first, end in cuts]
-            copies = fetch([(coef_in.at[a], coef_ref.at[a]) for a in at], sems)
+            rest_ref, both_ref, acc, pattern, block, sems = rest
+            late = [span for span in spans if span[0] >= split]
+            cuts = late[:-2] + [(late[-2][0], nbins)]
+            copies = fetch(
+                [
+                    (rest_in.at[pl.ds(first, end - first)], rest_ref.at[pl.ds(first - split, end - first)])
+                    for first, end in cuts
+                ],
+                sems,
+            )
+            waits = {first: c for (first, _), c in zip(cuts, copies)}
+            for i, head in enumerate(heads):
+                both_ref[i * HEAD : (i + 1) * HEAD] = head[:]
         else:
-            coef_ref, (acc, pattern, block) = coef_in, rest
+            rest_ref, (acc, pattern, block) = rest_in, rest
+            waits = {}
         lane = lax.broadcasted_iota(jnp.int32, (rows, LANES), 1)
         for g in range(count):
-            small = heads[g][:].astype(jnp.float32).T
+            operand, offset = sources[g]
+            small = heads[operand][offset : offset + HEAD].astype(jnp.float32).T
             value = jnp.zeros((rows, LANES), jnp.float32)
             where = jnp.zeros((rows, LANES), jnp.float32)
             for k in range(kbins):
@@ -100,15 +117,16 @@
             pattern[g * rows : (g + 1) * rows] = value.astype(pattern.dtype)
             block[g * rows : (g + 1) * rows] = where.astype(block.dtype)
 
-        for i, (first, end) in enumerate(spans):
+        for first, end in spans:
             parts = []
             for c in range(first // LANES, pl.cdiv(end, LANES)):
                 here = block[:] == jnp.asarray(c, block.dtype)
                 parts.append(jnp.where(here, pattern[:], jnp.zeros_like(pattern)).astype(jnp.bfloat16))
             weights = jnp.concatenate(parts, axis=1) if len(parts) > 1 else parts[0]
-            if stream and i < len(copies):
-                copies[i].wait()
-            part = jnp.dot(weights[:, : end - first], coef_ref[first:end], preferred_element_type=jnp.float32)
+            if first in waits:
+                waits[first].wait()
+            coef = first_ref[first:end] if first < split else rest_ref[first - split : end - split]
+            part = jnp.dot(weights[:, : end - first], coef, preferred_element_type=jnp.float32)
             acc[:] = part if first == 0 else acc[:] + part
 
         for g in range(count):
@@ -159,7 +177,7 @@
     return linear, square
 
 
-def near_kernel(masks):
+def first_kernel(masks):
     def kernel(me_ref, base_ref, closed_ref, target_ref, *refs):
         codes, out_ref = refs[:-1], refs[-1]
         zero = jnp.zeros(out_ref.shape[1:], jnp.float32)
@@ -168,15 +186,15 @@
     return kernel
 
 
-def far_kernel(masks):
-    def kernel(me_ref, base_ref, closed_ref, target_ref, near_ref, sums_ref, *refs):
+def second_kernel(masks, zones):
+    def kernel(me_ref, own_ref, base_ref, closed_ref, target_ref, first_ref, sums_ref, *refs):
         codes, out_ref = refs[:-1], refs[-1]
         linear, square = grad_terms(
-            me_ref, base_ref, closed_ref, target_ref, codes, masks, near_ref[0], near_ref[1]
+            me_ref, base_ref, closed_ref, target_ref, codes, masks, first_ref[0], first_ref[1]
         )
         lane = lax.broadcasted_iota(jnp.int32, sums_ref.shape, 1)
-        row = jnp.where(lane == 0, 2.0 * jnp.sum(linear, keepdims=True), sums_ref[:])
-        row = jnp.where(lane == 1, 2.0 * jnp.sum(square, keepdims=True), row)
+        row = jnp.where(lane == own_ref[0], 2.0 * jnp.sum(linear, keepdims=True), sums_ref[:])
+        row = jnp.where(lane == own_ref[0] + zones, 2.0 * jnp.sum(square, keepdims=True), row)
         out_ref[:] = jnp.broadcast_to(row[None], out_ref.shape)
 
     return kernel
@@ -185,29 +203,23 @@
 def last_kernel(groups, zones, windows):
     def kernel(place_ref, own_ref, heard_ref, zone_ref, area_ref, openness_ref, base_ref, closed_ref, *refs):
         codes, (lit_ref, step_ref) = refs[:groups], refs[groups:]
-        sums = heard_ref[0]
-        for z in range(1, zones):
-            sums = sums + heard_ref[z * groups]
-        zone = zone_ref[:]
-        chosen = jnp.zeros(zone.shape, jnp.float32)
-        square = jnp.zeros((1, 1), jnp.float32)
-        own_share = jnp.zeros((1, 1), jnp.float32)
-        for z in range(zones):
-            at = FRONT + 3 * z
-            num, den, squares = sums[:, at : at + 1], sums[:, at + 1 : at + 2], sums[:, at + 2 : at + 3]
-            share = num / den
-            both = jnp.sum(heard_ref[z * groups : (z + 1) * groups], axis=0)
-            ratio = (both[:, 0:1] + share * both[:, 1:2]) / den
-            square = square + ratio * ratio * squares
-            chosen = jnp.where(zone == z, ratio, chosen)
-            own_share = jnp.where(own_ref[0] == z, share, own_share)
-        rms = jnp.sqrt(square / windows + 1e-06)
-        step_ref[:] = jnp.clip(openness_ref[:] - 0.25 * (area_ref[:] * chosen) / rms, 0.0, 1.0)
+        total = jnp.sum(heard_ref[:], axis=0)
+        linear, quadratic, num, den, squares = [total[:, i * zones : (i + 1) * zones] for i in range(5)]
+        share = num / den
+        lane = lax.broadcasted_iota(jnp.int32, share.shape, 1)
+        own_share = jnp.sum(jnp.where(lane == own_ref[0], share, 0.0), keepdims=True)
         width = codes[0].shape[1]
         for mask in range(groups):
             at = place(place_ref, mask, width)
             lit = closed_ref[:, at] + own_share * cross_of(codes[mask], base_ref[:, at])
             lit_ref[:, at] = lit.astype(jnp.bfloat16)
+        ratio = groups * (linear + share * quadratic) / den
+        rms = jnp.sqrt(jnp.sum(ratio * ratio * squares, keepdims=True) / (windows * groups) + 1e-06)
+        zone = zone_ref[:]
+        chosen = jnp.zeros(zone.shape, jnp.float32)
+        for z in range(zones):
+            chosen = jnp.where(zone == z, ratio[:, z : z + 1], chosen)
+        step_ref[:] = jnp.clip(openness_ref[:] - 0.25 * (area_ref[:] * chosen) / rms, 0.0, 1.0)
 
     return kernel
 
@@ -225,7 +237,7 @@
     windows = area.shape[0]
     assert nbins % LANES == 0 or nbins % LANES >= 2 * kbins
     assert nbins <= 256 * LANES and width % LANES == 0 and windows % LANES == 0 and 3 * kbins <= HEAD
-    assert groups & (groups - 1) == 0 and groups > 1 and rows % 16 == 0
+    assert groups == 4 and rows % 16 == 0
     shape = jax.ShapeDtypeStruct
     f32, bf16 = jnp.float32, jnp.bfloat16
     dma = lambda n: pltpu.SemaphoreType.DMA((n,))
@@ -237,42 +249,43 @@
         in_specs=[HBM, HBM],
         scratch_shapes=[pltpu.VMEM((kbins, rows), jnp.int32), pltpu.VMEM((kbins, rows), bf16), dma(2)],
     )(sun_bins.T, sun_rad.T)
-    order = list(range(groups))[::-1]
-    heads = {mask: exchange(packed, "hour", mask) if mask else packed for mask in order}
+    heads = exchange(packed, "hour", 3)
 
     tiles = (windows // LANES, LANES)
-    message = pl.cdiv(FRONT + 3 * zones, LANES) * LANES
-    zone_sums, zone2, area2, openness2 = call(
-        sums_kernel(zones),
-        "sums",
-        [shape((1, message), f32), shape(tiles, jnp.int32), shape(tiles, f32), shape(tiles, f32)],
-        in_specs=[HBM] * 3,
-        out_specs=[VMEM] * 4,
-        scratch_shapes=[dma(3)],
-    )(zone_of.reshape(tiles), area.reshape(tiles), openness.reshape(tiles))
-
-    def sun(masks, coef, stream):
-        count = len(masks)
-        outs = [shape((rows + TAIL, width), jnp.int16)] * count
+    message = pl.cdiv(5 * zones, LANES) * LANES
+    split = nbins // 2 // (CHUNK * LANES) * CHUNK * LANES + CHUNK * LANES
+    assert split + 2 * CHUNK * LANES < nbins <= split + 3 * CHUNK * LANES
+    coef, zone_sums, zone2, area2, openness2 = call(
+        fetch_kernel(zones),
+        "fetch",
+        [shape((split, width), bf16), shape((1, message), f32)]
+        + [shape(tiles, jnp.int32), shape(tiles, f32), shape(tiles, f32)],
+        in_specs=[HBM] * 4,
+        out_specs=[VMEM] * 5,
+        scratch_shapes=[dma(4)],
+    )(sun_coef, zone_of.reshape(tiles), area.reshape(tiles), openness.reshape(tiles))
+
+    def sun(sources, rest, stream, *heads):
+        count = len(sources)
+        late = [shape((nbins - split, width), bf16), shape((2 * HEAD, rows), bf16)] if stream else []
         scratch = [pltpu.VMEM((count * rows, width), f32)] + [pltpu.VMEM((count * rows, LANES), PATTERN)] * 2
-        found = call(
-            sun_kernel(count, kbins, stream),
+        return call(
+            sun_kernel(sources, kbins, stream),
             "sun",
-            outs + [shape((nbins, width), bf16)] * stream,
-            flops=2 * count * rows * nbins * width * stream,
-            moved=2 * nbins * width * stream,
-            in_specs=[HBM if stream else VMEM] + [VMEM] * count,
-            out_specs=[VMEM] * (count + stream),
-            scratch_shapes=scratch + [dma(pl.cdiv(nbins, CHUNK * LANES))] * stream,
-        )(coef, *[heads[mask] for mask in masks])
-        return dict(zip(masks, found)), found[-1]
-
-    assert nbins > CHUNK * LANES
-    far, near = order[: groups // 2], order[groups // 2 :]
-    suns, coef = sun(far, sun_coef, 1)
-    codes = {mask: exchange(x, "hour", mask) for mask, x in suns.items()}
-    suns, _ = sun(near, coef, 0)
-    codes |= {mask: exchange(x, "hour", mask) if mask else x for mask, x in suns.items()}
+            [shape((rows + TAIL, width), jnp.int16)] * count + late,
+            in_specs=[VMEM, HBM if stream else VMEM] + [VMEM] * len(heads),
+            out_specs=[VMEM] * (count + len(late)),
+            scratch_shapes=scratch + ([dma(2)] if stream else []),
+        )(coef, rest, *heads)
+
+    codes = [None] * groups
+    code, late, both = sun([(1, 0)], sun_coef, True, packed, heads)
+    codes[3] = exchange(code, "hour", 3)
+    heads = exchange(both, "hour", 1)
+    (code,) = sun([(0, HEAD)], late, False, heads)
+    codes[2] = exchange(code, "hour", 2)
+    code, codes[0] = sun([(0, 0), (1, 0)], late, False, heads, packed)
+    codes[1] = exchange(code, "hour", 1)
 
     base, closed, wanted = call(
         base_kernel,
@@ -287,25 +300,26 @@
             dma(4),
         ],
     )(codes[0], sky.T, sky_open, sky_closed, target)
-    near_sums = call(
-        near_kernel(near),
-        "near",
+    first, second = [3, 2, 0], [1]
+    first_sums = call(
+        first_kernel(first),
+        "first",
         shape((2, 8, width), f32),
-        in_specs=[SMEM] + [VMEM] * (3 + len(near)),
-    )(me, base, closed, wanted, *[codes[mask] for mask in near])
+        in_specs=[SMEM] + [VMEM] * (3 + len(first)),
+    )(me, base, closed, wanted, *[codes[mask] for mask in first])
     sent = call(
-        far_kernel(far),
-        "far",
+        second_kernel(second, zones),
+        "second",
         shape((zones * groups, 1, message), f32),
-        in_specs=[SMEM] + [VMEM] * (5 + len(far)),
-    )(me, base, closed, wanted, near_sums, zone_sums, *[codes[mask] for mask in far])
+        in_specs=[SMEM] * 2 + [VMEM] * (5 + len(second)),
+    )(me, own_zone, base, closed, wanted, first_sums, zone_sums, *[codes[mask] for mask in second])
     heard = lax.all_to_all(sent, ("sens", "hour"), 0, 0)
     illuminance, new_openness = call(
         last_kernel(groups, zones, windows * zones),
         "last",
         [shape((rows, sensors), bf16), shape(tiles, f32)],
         in_specs=[SMEM] * 2 + [VMEM] * (6 + groups),
-    )(me, own_zone, heard, zone2, area2, openness2, base, closed, *[codes[mask] for mask in range(groups)])
+    )(me, own_zone, heard, zone2, area2, openness2, base, closed, *codes)
     return (illuminance, new_openness.reshape(-1))
 
 

time: 45 us -> 40.6 us (0.902)
  waiting for transfers between devices: 18.7 us -> 2.63 us
  blocking collectives: 0 us -> 11.3 us
  starting transfers between devices: 12.7 us -> 13.6 us
  Pallas kernels: 12.6 us -> 12.1 us
    all_to_all x0 -> x1, blocking collectives: none -> 11.3 us  [local(): heard = lax.all_to_all(sent, ('sens', 'hour'), 0, 0)]
    ppermute x6 -> x5, waiting for transfers between devices: 11.6 us -> 2.63 us  [exchange(): lax.ppermute(x, axis, [(i, i ^ mask) for i in range(lax.axis_size(axis))])]
    all_to_all x1 -> x0, waiting for transfers between devices: 7.09 us -> none  [local(): heard = lax.all_to_all(sent, ('sens', 'hour'), 0, 0)]
    ppermute x6 -> x5, starting transfers between devices: 9.3 us -> 13.6 us  [exchange(): lax.ppermute(x, axis, [(i, i ^ mask) for i in range(lax.axis_size(axis))])]
    all_to_all x1 -> x0, starting transfers between devices: 3.44 us -> none  [local(): heard = lax.all_to_all(sent, ('sens', 'hour'), 0, 0)]
    pallas_call x8 -> x9, Pallas kernels: 12.6 us -> 12.1 us  [call(): run(*[pltpu.with_memory_space_constraint(x, pltpu.HBM) if s is HBM else x...]
  transfers between devices with their start and end apart: 7 -> 5, of which waited for: 6 -> 3; matrix products, arithmetic and copies ran while one was open for 0% -> 0% of each run, Pallas kernels for 15% -> 19%
where the time goes in v1:
time: 40.6 us; the launch traced here: 40.3 us
  starting transfers between devices  13.6 us (33%)
  Pallas kernels  12.1 us (30%)
  blocking collectives  11.3 us (28%)
  waiting for transfers between devices  2.63 us (6%)
  between operations  0.71 us (2%)
    ppermute x5, starting transfers between devices, exchange(): lax.ppermute(x, axis, [(i, i ^ mask) for i in range(lax.axis_size(axis))])  13.6 us
    pallas_call x9, Pallas kernels, call(): run(*[pltpu.with_memory_space_constraint(x, pltpu.HBM) if s is HBM else x...  12.1 us
    all_to_all x1, blocking collectives, local(): heard = lax.all_to_all(sent, ('sens', 'hour'), 0, 0)  11.3 us
    ppermute x5, waiting for transfers between devices, exchange(): lax.ppermute(x, axis, [(i, i ^ mask) for i in range(lax.axis_size(axis))])  2.63 us
  transfers between devices with their start and end apart: 5, of which 3 were waited for; matrix products, arithmetic and copies ran while one was open for 0% of the time, Pallas kernels for 19%

profile of v1, /device:TPU:0, one launch (start us, length us, event | category | flops | bytes accessed | tf_op | source)
XLA Modules:
  0.0 40.3 jit_solution(17647172581982601798)
XLA Ops:
  0.6 0.7 %pack.1.refs_0_.refs_1_ = bf16[16,128]{1,0:T(8,128)(2,1)S(1)} custom-call(s32[4,128]{1,0:T(4,128)} %bitcast.13, bf16[4,128]{1,0:T(4,128)(2,1)} %bitcast.14), custom_call_target="tpu_custom_call" | custom-call | tf_op jit(solution)/shard_map/pack/pallas_call | solution.py:31
  1.4 5.1 %collective-permute-start = (bf16[16,128]{1,0:T(8,128)(2,1)S(1)}, bf16[16,128]{1,0:T(8,128)(2,1)S(1)}, u32[]{:S(2)}, u32[]{:S(2)}) collective-permute-start(bf16[16,128]{1,0:T(8,128)(2,1)S(1)} %pack.1.refs_0_.refs_1_), channel_id=1, source_target_pairs={{0,3},{1,2},{2,1},{3,0},{4,7},{5,6},{6,5},{7,4},{8,11},{9,10},{10,... | collective-permute-start | bytes 12296 | tf_op jit(solution)/shard_map/ppermute | solution.py:37
  6.5 2.0 %fetch.1 = (bf16[3072,512]{1,0:T(8,128)(2,1)S(1)}, f32[1,128]{1,0:T(1,128)S(1)}, s32[8,128]{1,0:T(8,128)S(1)}, f32[8,128]{1,0:T(8,128)S(1)}, f32[8,128]{1,0:T(8,128)S(1)}) custom-call(bf16[5165,512]{1,0:T(8,128)(2,1)} %rest_in.1, s32[8,128]{1,0:T(8,128)} %bitcast.10, f32[8,128]{1,0:T(8,128)} %bitcast.11, f32[8,128]{1,0:T(8,128)} %bitcast.12), custom_call_target="tpu_custom_call" | custom-call | tf_op jit(solution)/shard_map/fetch/pallas_call | solution.py:31
  8.5 0.0 collective-permute-done.refs_1_
  8.5 2.0 %sun.3 = (s16[136,512]{1,0:T(8,128)(2,1)S(1)}, bf16[2093,512]{1,0:T(8,128)(2,1)S(1)}, bf16[32,128]{1,0:T(8,128)(2,1)S(1)}) custom-call(bf16[3072,512]{1,0:T(8,128)(2,1)S(1)} %get-tuple-element.17.first_ref, bf16[5165,512]{1,0:T(8,128)(2,1)} %rest_in.1, bf16[16,128]{1,0:T(8,128)(2,1)S(1)} %pack.1.refs_0_.refs_1_, bf16[16,128]{1,0:T(8,128)(2,1)S(1)} %collective-permute-done.refs_1_), custom_call_target="tpu_custom_call" | custom-call | tf_op jit(solution)/shard_map/sun/pallas_call | solution.py:31
  10.5 0.1 collective-permute-start.1
  10.5 3.5 %collective-permute-start.2 = (s16[136,512]{1,0:T(8,128)(2,1)S(1)}, s16[136,512]{1,0:T(8,128)(2,1)S(1)}, u32[]{:S(2)}, u32[]{:S(2)}) collective-permute-start(s16[136,512]{1,0:T(8,128)(2,1)S(1)} %get-tuple-element.24), channel_id=1, source_target_pairs={{0,3},{1,2},{2,1},{3,0},{4,7},{5,6},{6,5},{7,4},{8,11},{9,10},{10,... | collective-permute-start | bytes 417800 | tf_op jit(solution)/shard_map/ppermute | solution.py:37
  14.0 0.2 collective-permute-done.1.refs_0_
  14.2 1.3 %sun.5 = s16[136,512]{1,0:T(8,128)(2,1)S(1)} custom-call(bf16[3072,512]{1,0:T(8,128)(2,1)S(1)} %get-tuple-element.17.first_ref, bf16[2093,512]{1,0:T(8,128)(2,1)S(1)} %get-tuple-element.18.rest_in, bf16[32,128]{1,0:T(8,128)(2,1)S(1)} %collective-permute-done.1.refs_0_), custom_call_target="tpu_custom_call" | custom-call | tf_op jit(solution)/shard_map/sun/pallas_call | solution.py:31
  15.5 2.1 %collective-permute-start.3 = (s16[136,512]{1,0:T(8,128)(2,1)S(1)}, s16[136,512]{1,0:T(8,128)(2,1)S(1)}, u32[]{:S(2)}, u32[]{:S(2)}) collective-permute-start(s16[136,512]{1,0:T(8,128)(2,1)S(1)} %sun.5), channel_id=1, source_target_pairs={{0,2},{1,3},{2,0},{3,1},{4,6},{5,7},{6,4},{7,5},{8,10},{9,11},{10,... | collective-permute-start | bytes 417800 | tf_op jit(solution)/shard_map/ppermute | solution.py:37
  17.6 2.2 %sun.4 = (s16[136,512]{1,0:T(8,128)(2,1)S(1)}, s16[136,512]{1,0:T(8,128)(2,1)S(1)}) custom-call(bf16[3072,512]{1,0:T(8,128)(2,1)S(1)} %get-tuple-element.17.first_ref, bf16[2093,512]{1,0:T(8,128)(2,1)S(1)} %get-tuple-element.18.rest_in, bf16[32,128]{1,0:T(8,128)(2,1)S(1)} %collective-permute-done.1.refs_0_, bf16[16,128]{1,0:T(8,128)(2,1)S(1)} %pack.1.refs_0_.refs_1_), custom_call_target="tpu_custom_call" | custom-call | tf_op jit(solution)/shard_map/sun/pallas_call | solution.py:31
  19.8 2.8 %collective-permute-start.4 = (s16[136,512]{1,0:T(8,128)(2,1)S(1)}, s16[136,512]{1,0:T(8,128)(2,1)S(1)}, u32[]{:S(2)}, u32[]{:S(2)}) collective-permute-start(s16[136,512]{1,0:T(8,128)(2,1)S(1)} %get-tuple-element.26), channel_id=1, source_target_pairs={{0,1},{1,0},{2,3},{3,2},{4,5},{5,4},{6,7},{7,6},{8,9},{9,8},{10,11... | collective-permute-start | bytes 417800 | tf_op jit(solution)/shard_map/ppermute | solution.py:37
  22.6 1.8 %base.1 = (f32[128,2048]{1,0:T(8,128)S(1)}, f32[128,2048]{1,0:T(8,128)S(1)}, bf16[128,2048]{1,0:T(8,128)(2,1)S(1)}) custom-call(s16[136,512]{1,0:T(8,128)(2,1)S(1)} %get-tuple-element.20.token.refs_2_.refs_0_, bf16[146,128]{1,0:T(8,128)(2,1)} %bitcast.9, bf16[146,2048]{1,0:T(8,128)(2,1)} %open_hbm.1, bf16[146,2048]{1,0:T(8,128)(2,1)} %closed_hbm.1, ...), custom_call_target="tpu_custom_call" | custom-call | tf_op jit(solution)/shard_map/base/pallas_call | solution.py:31
  24.4 0.0 collective-permute-done.2.refs_0_.refs_3_
  24.4 1.5 %collective-permute-done.3.refs_1_.refs_2_ = s16[136,512]{1,0:T(8,128)(2,1)S(1)} collective-permute-done((s16[136,512]{1,0:T(8,128)(2,1)S(1)}, s16[136,512]{1,0:T(8,128)(2,1)S(1)}, u32[]{:S(2)}, u32[]{:S(2)}) %collective-permute-start.3) | collective-permute-done | bytes 139296 | tf_op jit(solution)/shard_map/ppermute | solution.py:37
  25.9 0.4 first.1.first_ref
  26.3 1.0 %collective-permute-done.4.refs_0_.refs_1_ = s16[136,512]{1,0:T(8,128)(2,1)S(1)} collective-permute-done((s16[136,512]{1,0:T(8,128)(2,1)S(1)}, s16[136,512]{1,0:T(8,128)(2,1)S(1)}, u32[]{:S(2)}, u32[]{:S(2)}) %collective-permute-start.4) | collective-permute-done | bytes 139296 | tf_op jit(solution)/shard_map/ppermute | solution.py:37
  27.3 0.3 second.1
  27.6 11.3 %all_to_all.5.heard_ref = f32[32,1,128]{2,1,0:T(1,128)S(1)} all-to-all(f32[32,1,128]{2,1,0:T(1,128)S(1)} %second.1), channel_id=1, replica_groups=mesh['sens'=8,'hour'=4] {'sens','hour'}, dimensions={0} | all-to-all | bytes 32768 | tf_op jit(solution)/shard_map/all_to_all | solution.py:316
  38.9 1.4 %last.1 = (bf16[128,2048]{1,0:T(8,128)(2,1)}, f32[8,128]{1,0:T(8,128)}) custom-call(s32[1]{0:T(128)} %bitcast.me_ref.place_ref, s32[1]{0:T(128)} %bitcast.1.own_ref, f32[32,1,128]{2,1,0:T(1,128)S(1)} %all_to_all.5.heard_ref, s32[8,128]{1,0:T(8,128)S(1)} %get-tuple-element.27.zone_ref, f32[8,128]{1,0:T(8,128)S(1)} %get-tuple-element.28.area_ref, ...), custom_call_target="tpu_custom_call" | custom-call | tf_op jit(solution)/shard_map/last/pallas_call | solution.py:31
Async XLA Ops:
  1.4 7.1 %collective-permute-start = (bf16[16,128]{1,0:T(8,128)(2,1)S(1)}, bf16[16,128]{1,0:T(8,128)(2,1)S(1)}, u32[]{:S(2)}, u32[]{:S(2)}) collective-permute-start(bf16[16,128]{1,0:T(8,128)(2,1)S(1)} %pack.1.refs_0_.refs_1_), channel_id=1, source_target_pairs={{0,3},{1,2},{2,1},{3,0},{4,7},{5,6},{6,5},{7,4},{8,11},{9,10},{10,... | collective-permute-start | bytes 12296 | tf_op jit(solution)/shard_map/ppermute | solution.py:37
  10.5 3.7 %collective-permute-start.1 = (bf16[32,128]{1,0:T(8,128)(2,1)S(1)}, bf16[32,128]{1,0:T(8,128)(2,1)S(1)}, u32[]{:S(2)}, u32[]{:S(2)}) collective-permute-start(bf16[32,128]{1,0:T(8,128)(2,1)S(1)} %get-tuple-element.19), channel_id=1, source_target_pairs={{0,1},{1,0},{2,3},{3,2},{4,5},{5,4},{6,7},{7,6},{8,9},{9,8},{10,11... | collective-permute-start | bytes 24584 | tf_op jit(solution)/shard_map/ppermute | solution.py:37
  10.5 13.9 %collective-permute-start.2 = (s16[136,512]{1,0:T(8,128)(2,1)S(1)}, s16[136,512]{1,0:T(8,128)(2,1)S(1)}, u32[]{:S(2)}, u32[]{:S(2)}) collective-permute-start(s16[136,512]{1,0:T(8,128)(2,1)S(1)} %get-tuple-element.24), channel_id=1, source_target_pairs={{0,3},{1,2},{2,1},{3,0},{4,7},{5,6},{6,5},{7,4},{8,11},{9,10},{10,... | collective-permute-start | bytes 417800 | tf_op jit(solution)/shard_map/ppermute | solution.py:37
  15.5 10.4 %collective-permute-start.3 = (s16[136,512]{1,0:T(8,128)(2,1)S(1)}, s16[136,512]{1,0:T(8,128)(2,1)S(1)}, u32[]{:S(2)}, u32[]{:S(2)}) collective-permute-start(s16[136,512]{1,0:T(8,128)(2,1)S(1)} %sun.5), channel_id=1, source_target_pairs={{0,2},{1,3},{2,0},{3,1},{4,6},{5,7},{6,4},{7,5},{8,10},{9,11},{10,... | collective-permute-start | bytes 417800 | tf_op jit(solution)/shard_map/ppermute | solution.py:37
  19.8 7.5 %collective-permute-start.4 = (s16[136,512]{1,0:T(8,128)(2,1)S(1)}, s16[136,512]{1,0:T(8,128)(2,1)S(1)}, u32[]{:S(2)}, u32[]{:S(2)}) collective-permute-start(s16[136,512]{1,0:T(8,128)(2,1)S(1)} %get-tuple-element.26), channel_id=1, source_target_pairs={{0,1},{1,0},{2,3},{3,2},{4,5},{5,4},{6,7},{7,6},{8,9},{9,8},{10,11... | collective-permute-start | bytes 417800 | tf_op jit(solution)/shard_map/ppermute | solution.py:37

commit v2 on v1

--- a/solution.py
+++ b/solution.py
@@ -44,14 +44,24 @@
     return copies
 
 
-def pack_kernel(bins_hbm, rad_hbm, out_ref, bins_ref, rad_ref, sems):
-    for c in fetch([(bins_hbm, bins_ref), (rad_hbm, rad_ref)], sems):
-        c.wait()
+def pack_kernel(me_ref, bins_hbm, rad_hbm, sky_hbm, target_hbm, out_ref, far_ref, bins_ref, rad_ref, sky_ref, sems):
+    rows, width = target_hbm.shape[0], far_ref.shape[1]
+    pairs = [(bins_hbm, bins_ref), (rad_hbm, rad_ref), (sky_hbm, sky_ref)]
+    copies = fetch(pairs + [(target_hbm.at[:, place(me_ref, 3, width)], far_ref.at[pl.ds(0, rows)])], sems)
+    copies[0].wait()
+    copies[1].wait()
     bins = bins_ref[:]
     kbins = bins.shape[0]
     fill = jnp.zeros((HEAD - 3 * kbins, bins.shape[1]), jnp.float32)
     parts = [rad_ref[:].astype(jnp.float32), (bins // LANES).astype(jnp.float32), (bins % LANES).astype(jnp.float32)]
     out_ref[:] = jnp.concatenate(parts + [fill], axis=0).astype(jnp.bfloat16)
+    copies[2].wait()
+    part = far_ref.shape[0] - rows
+    far_ref[rows:] = jnp.zeros((part, width), far_ref.dtype)
+    for c in range(pl.cdiv(sky_ref.shape[0], part)):
+        some = sky_ref[c * part : (c + 1) * part]
+        far_ref[rows : rows + some.shape[0], c * rows : (c + 1) * rows] = some
+    copies[3].wait()
 
 
 def fetch_kernel(zones):
@@ -75,7 +85,7 @@
     return kernel
 
 
-def sun_kernel(sources, kbins, stream):
+def sun_kernel(sources, kbins, stream, plain):
     count = len(sources)
     inputs = 1 + max(operand for operand, _ in sources)
 
@@ -101,7 +111,7 @@
             for i, head in enumerate(heads):
                 both_ref[i * HEAD : (i + 1) * HEAD] = head[:]
         else:
-            rest_ref, (acc, pattern, block) = rest_in, rest
+            rest_ref, (plain_ref, acc, pattern, block) = rest_in, rest
             waits = {}
         lane = lax.broadcasted_iota(jnp.int32, (rows, LANES), 1)
         for g in range(count):
@@ -131,6 +141,8 @@
 
         for g in range(count):
             sun = acc[g * rows : (g + 1) * rows]
+            if plain == g:
+                plain_ref[:] = sun
             power = jnp.ceil(jnp.log2(jnp.maximum(jnp.max(sun, axis=0, keepdims=True), 1e-30)))
             code = jnp.round(sun * (LEVELS / jnp.exp2(power)) - 0.5 * LEVELS)
             outs[g][:rows] = code.astype(jnp.int32).astype(jnp.int16)
@@ -140,19 +152,34 @@
     return kernel
 
 
-def base_kernel(
-    token, sky_hbm, open_hbm, closed_hbm, target_hbm, cross_ref, closed_out, target_out, sky_ref, open_ref, closed_ref, sems
-):
-    pairs = [(sky_hbm, sky_ref), (open_hbm, open_ref), (closed_hbm, closed_ref), (target_hbm, target_out)]
-    copies = fetch(pairs, sems)
-    for c in copies[:3]:
-        c.wait()
-    over = (((0,), (0,)), ((), ()))
-    closed = lax.dot_general(sky_ref[:], closed_ref[:], over, preferred_element_type=jnp.float32)
-    opened = lax.dot_general(sky_ref[:], open_ref[:], over, preferred_element_type=jnp.float32)
-    closed_out[:] = closed
-    cross_ref[:] = opened - closed
-    copies[3].wait()
+def base_kernel(patches):
+    def kernel(
+        me_ref, far_ref, sun_ref, code_ref, sky_hbm, open_hbm, closed_hbm, target_hbm,
+        cross_ref, closed_out, target_out, sums_ref, code_out, sky_ref, open_ref, closed_ref, sems,
+    ):
+        pairs = [(sky_hbm, sky_ref), (open_hbm, open_ref), (closed_hbm, closed_ref), (target_hbm, target_out)]
+        copies = fetch(pairs, sems)
+        code_out[:] = code_ref[:]
+        rows, width = sun_ref.shape
+        part = far_ref.shape[0] - rows
+        blocks = [far_ref[rows:, c * rows : (c + 1) * rows] for c in range(pl.cdiv(patches, part))]
+        far_sky = jnp.concatenate(blocks, axis=0)[:patches]
+        for c in copies[:3]:
+            c.wait()
+        over = (((0,), (0,)), ((), ()))
+        dot = lambda x, y: lax.dot_general(x, y, over, preferred_element_type=jnp.float32)
+        own = place(me_ref, 0, width)
+        closed = dot(far_sky, closed_ref[:, own])
+        cross = dot(far_sky, open_ref[:, own]) - closed + sun_ref[:]
+        apart = closed - far_ref[:rows].astype(jnp.float32)
+        sums_ref[0] = jnp.sum((apart * cross).reshape(rows // 8, 8, width), axis=0)
+        sums_ref[1] = jnp.sum((cross * cross).reshape(rows // 8, 8, width), axis=0)
+        closed = dot(sky_ref[:], closed_ref[:])
+        closed_out[:] = closed
+        cross_ref[:] = dot(sky_ref[:], open_ref[:]) - closed
+        copies[3].wait()
+
+    return kernel
 
 
 def place(me_ref, mask, width):
@@ -178,10 +205,11 @@
 
 
 def first_kernel(masks):
-    def kernel(me_ref, base_ref, closed_ref, target_ref, *refs):
+    def kernel(me_ref, base_ref, closed_ref, target_ref, sums_ref, *refs):
         codes, out_ref = refs[:-1], refs[-1]
-        zero = jnp.zeros(out_ref.shape[1:], jnp.float32)
-        out_ref[0], out_ref[1] = grad_terms(me_ref, base_ref, closed_ref, target_ref, codes, masks, zero, zero)
+        out_ref[0], out_ref[1] = grad_terms(
+            me_ref, base_ref, closed_ref, target_ref, codes, masks, sums_ref[0], sums_ref[1]
+        )
 
     return kernel
 
@@ -242,14 +270,23 @@
     f32, bf16 = jnp.float32, jnp.bfloat16
     dma = lambda n: pltpu.SemaphoreType.DMA((n,))
 
-    packed = call(
+    part = -(-pl.cdiv(patches, width // rows) // 8) * 8
+    assert rows == LANES and patches <= part * (width // rows)
+    packed, far = call(
         pack_kernel,
         "pack",
-        shape((HEAD, rows), bf16),
-        in_specs=[HBM, HBM],
-        scratch_shapes=[pltpu.VMEM((kbins, rows), jnp.int32), pltpu.VMEM((kbins, rows), bf16), dma(2)],
-    )(sun_bins.T, sun_rad.T)
-    heads = exchange(packed, "hour", 3)
+        [shape((HEAD, rows), bf16), shape((rows + part, width), bf16)],
+        in_specs=[SMEM] + [HBM] * 4,
+        out_specs=[VMEM] * 2,
+        scratch_shapes=[
+            pltpu.VMEM((kbins, rows), jnp.int32),
+            pltpu.VMEM((kbins, rows), bf16),
+            pltpu.VMEM((patches, rows), bf16),
+            dma(4),
+        ],
+    )(me, sun_bins.T, sun_rad.T, sky.T, target)
+    heads = exchange(packed, "hour", 2)
+    far = exchange(far, "hour", 3)
 
     tiles = (windows // LANES, LANES)
     message = pl.cdiv(5 * zones, LANES) * LANES
@@ -267,10 +304,11 @@
 
     def sun(sources, rest, stream, *heads):
         count = len(sources)
-        late = [shape((nbins - split, width), bf16), shape((2 * HEAD, rows), bf16)] if stream else []
+        late = [shape((nbins - split, width), bf16), shape((2 * HEAD, rows), bf16)]
+        late = late if stream else [shape((rows, width), f32)]
         scratch = [pltpu.VMEM((count * rows, width), f32)] + [pltpu.VMEM((count * rows, LANES), PATTERN)] * 2
         return call(
-            sun_kernel(sources, kbins, stream),
+            sun_kernel(sources, kbins, stream, None if stream else 0),
             "sun",
             [shape((rows + TAIL, width), jnp.int16)] * count + late,
             in_specs=[VMEM, HBM if stream else VMEM] + [VMEM] * len(heads),
@@ -280,33 +318,33 @@
 
     codes = [None] * groups
     code, late, both = sun([(1, 0)], sun_coef, True, packed, heads)
-    codes[3] = exchange(code, "hour", 3)
+    codes[2] = exchange(code, "hour", 2)
     heads = exchange(both, "hour", 1)
-    (code,) = sun([(0, HEAD)], late, False, heads)
-    codes[2] = exchange(code, "hour", 2)
-    code, codes[0] = sun([(0, 0), (1, 0)], late, False, heads, packed)
+    far_code, code, codes[0], far_sun = sun([(0, HEAD), (0, 0), (1, 0)], late, False, heads, packed)
     codes[1] = exchange(code, "hour", 1)
 
-    base, closed, wanted = call(
-        base_kernel,
+    base, closed, wanted, far_sums, far_code = call(
+        base_kernel(patches),
         "base",
-        [shape((rows, sensors), f32)] * 2 + [shape((rows, sensors), bf16)],
-        in_specs=[ANY] + [HBM] * 4,
-        out_specs=[VMEM] * 3,
+        [shape((rows, sensors), f32)] * 2
+        + [shape((rows, sensors), bf16), shape((2, 8, width), f32), shape(far_code.shape, jnp.int16)],
+        in_specs=[SMEM] + [VMEM] * 3 + [HBM] * 4,
+        out_specs=[VMEM] * 5,
         scratch_shapes=[
             pltpu.VMEM((patches, rows), bf16),
             pltpu.VMEM((patches, sensors), bf16),
             pltpu.VMEM((patches, sensors), bf16),
             dma(4),
         ],
-    )(codes[0], sky.T, sky_open, sky_closed, target)
-    first, second = [3, 2, 0], [1]
+    )(me, far, far_sun, far_code, sky.T, sky_open, sky_closed, target)
+    codes[3] = exchange(far_code, "hour", 3)
+    first, second = [2, 0], [1]
     first_sums = call(
         first_kernel(first),
         "first",
         shape((2, 8, width), f32),
-        in_specs=[SMEM] + [VMEM] * (3 + len(first)),
-    )(me, base, closed, wanted, *[codes[mask] for mask in first])
+        in_specs=[SMEM] + [VMEM] * (4 + len(first)),
+    )(me, base, closed, wanted, far_sums, *[codes[mask] for mask in first])
     sent = call(
         second_kernel(second, zones),
         "second",

time: 40.6 us -> 43.3 us (1.067)
  waiting for transfers between devices: 2.63 us -> 6.1 us
  starting transfers between devices: 13.6 us -> 10.7 us
  blocking collectives: 11.3 us -> 12.8 us
  Pallas kernels: 12.1 us -> 12.7 us
    ppermute x5 -> x6, waiting for transfers between devices: 2.63 us -> 6.1 us  [exchange(): lax.ppermute(x, axis, [(i, i ^ mask) for i in range(lax.axis_size(axis))])]
    ppermute x5 -> x6, starting transfers between devices: 13.6 us -> 10.7 us  [exchange(): lax.ppermute(x, axis, [(i, i ^ mask) for i in range(lax.axis_size(axis))])]
    all_to_all x1, blocking collectives: 11.3 us -> 12.8 us  [local(): heard = lax.all_to_all(sent, ('sens', 'hour'), 0, 0)]
    pallas_call x9 -> x8, Pallas kernels: 12.1 us -> 12.7 us  [call(): run(*[pltpu.with_memory_space_constraint(x, pltpu.HBM) if s is HBM else x...]
  transfers between devices with their start and end apart: 5 -> 6, of which waited for: 3 -> 2; matrix products, arithmetic and copies ran while one was open for 0% -> 0% of each run, Pallas kernels for 19% -> 24%
where the time goes in v2:
time: 43.3 us; the launch traced here: 43 us
  blocking collectives  12.8 us (30%)
  Pallas kernels  12.7 us (29%)
  starting transfers between devices  10.7 us (25%)
  waiting for transfers between devices  6.1 us (14%)
  between operations  0.72 us (2%)
    all_to_all x1, blocking collectives, local(): heard = lax.all_to_all(sent, ('sens', 'hour'), 0, 0)  12.8 us
    pallas_call x8, Pallas kernels, call(): run(*[pltpu.with_memory_space_constraint(x, pltpu.HBM) if s is HBM else x...  12.7 us
    ppermute x6, starting transfers between devices, exchange(): lax.ppermute(x, axis, [(i, i ^ mask) for i in range(lax.axis_size(axis))])  10.7 us
    ppermute x6, waiting for transfers between devices, exchange(): lax.ppermute(x, axis, [(i, i ^ mask) for i in range(lax.axis_size(axis))])  6.1 us
  transfers between devices with their start and end apart: 6, of which 2 were waited for; matrix products, arithmetic and copies ran while one was open for 0% of the time, Pallas kernels for 24%

profile of v2, /device:TPU:0, one launch (start us, length us, event | category | flops | bytes accessed | tf_op | source)
XLA Modules:
  0.0 43.0 jit_solution(3552372698895951342)
XLA Ops:
  0.6 1.0 %pack.1 = (bf16[16,128]{1,0:T(8,128)(2,1)S(1)}, bf16[168,512]{1,0:T(8,128)(2,1)S(1)}) custom-call(s32[1]{0:T(128)} %bitcast.me_ref.place_ref, s32[4,128]{1,0:T(4,128)} %bitcast.14, bf16[4,128]{1,0:T(4,128)(2,1)} %bitcast.15, bf16[146,128]{1,0:T(8,128)(2,1)} %bitcast.9, bf16[128,2048]{1,0:T(8,128)(2,1)} %target_hbm.3), custom_call_target="tpu_custom_call" | custom-call | tf_op jit(solution)/shard_map/pack/pallas_call | solution.py:31
  1.6 5.1 %collective-permute-start = (bf16[168,512]{1,0:T(8,128)(2,1)S(1)}, bf16[168,512]{1,0:T(8,128)(2,1)S(1)}, u32[]{:S(2)}, u32[]{:S(2)}) collective-permute-start(bf16[168,512]{1,0:T(8,128)(2,1)S(1)} %get-tuple-element.23), channel_id=1, source_target_pairs={{0,3},{1,2},{2,1},{3,0},{4,7},{5,6},{6,5},{7,4},{8,11},{9,10},{10,... | collective-permute-start | bytes 516104 | tf_op jit(solution)/shard_map/ppermute | solution.py:37
  6.8 0.0 collective-permute-start.1
  6.8 2.0 %fetch.1 = (bf16[3072,512]{1,0:T(8,128)(2,1)S(1)}, f32[1,128]{1,0:T(1,128)S(1)}, s32[8,128]{1,0:T(8,128)S(1)}, f32[8,128]{1,0:T(8,128)S(1)}, f32[8,128]{1,0:T(8,128)S(1)}) custom-call(bf16[5165,512]{1,0:T(8,128)(2,1)} %rest_in.1, s32[8,128]{1,0:T(8,128)} %bitcast.11, f32[8,128]{1,0:T(8,128)} %bitcast.12, f32[8,128]{1,0:T(8,128)} %bitcast.13), custom_call_target="tpu_custom_call" | custom-call | tf_op jit(solution)/shard_map/fetch/pallas_call | solution.py:31
  8.7 5.4 %collective-permute-done.1.refs_1_ = bf16[16,128]{1,0:T(8,128)(2,1)S(1)} collective-permute-done((bf16[16,128]{1,0:T(8,128)(2,1)S(1)}, bf16[16,128]{1,0:T(8,128)(2,1)S(1)}, u32[]{:S(2)}, u32[]{:S(2)}) %collective-permute-start.1) | collective-permute-done | bytes 4128 | tf_op jit(solution)/shard_map/ppermute | solution.py:37
  14.1 2.0 %sun.2 = (s16[136,512]{1,0:T(8,128)(2,1)S(1)}, bf16[2093,512]{1,0:T(8,128)(2,1)S(1)}, bf16[32,128]{1,0:T(8,128)(2,1)S(1)}) custom-call(bf16[3072,512]{1,0:T(8,128)(2,1)S(1)} %get-tuple-element.24.first_ref, bf16[5165,512]{1,0:T(8,128)(2,1)} %rest_in.1, bf16[16,128]{1,0:T(8,128)(2,1)S(1)} %get-tuple-element.25.refs_0_.refs_1_, ...), custom_call_target="tpu_custom_call" | custom-call | tf_op jit(solution)/shard_map/sun/pallas_call | solution.py:31
  16.1 0.1 collective-permute-start.2
  16.2 3.0 %collective-permute-start.3 = (s16[136,512]{1,0:T(8,128)(2,1)S(1)}, s16[136,512]{1,0:T(8,128)(2,1)S(1)}, u32[]{:S(2)}, u32[]{:S(2)}) collective-permute-start(s16[136,512]{1,0:T(8,128)(2,1)S(1)} %get-tuple-element.34), channel_id=1, source_target_pairs={{0,2},{1,3},{2,0},{3,1},{4,6},{5,7},{6,4},{7,5},{8,10},{9,11},{10,... | collective-permute-start | bytes 417800 | tf_op jit(solution)/shard_map/ppermute | solution.py:37
  19.3 0.7 %collective-permute-done.2.refs_0_ = bf16[32,128]{1,0:T(8,128)(2,1)S(1)} collective-permute-done((bf16[32,128]{1,0:T(8,128)(2,1)S(1)}, bf16[32,128]{1,0:T(8,128)(2,1)S(1)}, u32[]{:S(2)}, u32[]{:S(2)}) %collective-permute-start.2) | collective-permute-done | bytes 8224 | tf_op jit(solution)/shard_map/ppermute | solution.py:37
  19.9 3.2 %sun.3 = (s16[136,512]{1,0:T(8,128)(2,1)S(1)}, s16[136,512]{1,0:T(8,128)(2,1)S(1)}, s16[136,512]{1,0:T(8,128)(2,1)S(1)}, f32[128,512]{1,0:T(8,128)S(1)}) custom-call(bf16[3072,512]{1,0:T(8,128)(2,1)S(1)} %get-tuple-element.24.first_ref, bf16[2093,512]{1,0:T(8,128)(2,1)S(1)} %get-tuple-element.26.rest_in, bf16[32,128]{1,0:T(8,128)(2,1)S(1)} %collective-permute-done.2.refs_0_, ...), custom_call_target="tpu_custom_call" | custom-call | tf_op jit(solution)/shard_map/sun/pallas_call | solution.py:31
  23.1 0.1 collective-permute-start.4
  23.2 0.0 collective-permute-done.far_ref
  23.2 2.6 %base.1 = (f32[128,2048]{1,0:T(8,128)S(1)}, f32[128,2048]{1,0:T(8,128)S(1)}, bf16[128,2048]{1,0:T(8,128)(2,1)S(1)}, f32[2,8,512]{2,1,0:T(8,128)S(1)}, s16[136,512]{1,0:T(8,128)(2,1)}) custom-call(s32[1]{0:T(128)} %bitcast.me_ref.place_ref, bf16[168,512]{1,0:T(8,128)(2,1)S(1)} %collective-permute-done.far_ref, f32[128,512]{1,0:T(8,128)S(1)} %get-tuple-element.28.sun_ref, ...), custom_call_target="tpu_custom_call" | custom-call | tf_op jit(solution)/shard_map/base/pallas_call | solution.py:31
  25.8 2.5 %collective-permute-start.5 = (s16[136,512]{1,0:T(8,128)(2,1)}, s16[136,512]{1,0:T(8,128)(2,1)S(1)}, u32[]{:S(2)}, u32[]{:S(2)}) collective-permute-start(s16[136,512]{1,0:T(8,128)(2,1)} %get-tuple-element.41), channel_id=1, source_target_pairs={{0,3},{1,2},{2,1},{3,0},{4,7},{5,6},{6,5},{7,4},{8,11},{9,10},{10,... | collective-permute-start | bytes 417800 | tf_op jit(solution)/shard_map/ppermute | solution.py:37
  28.3 0.0 collective-permute-done.3.refs_0_.refs_2_
  28.3 0.2 first.1.first_ref
  28.5 0.0 collective-permute-done.4.refs_0_.refs_1_
  28.5 0.3 second.1
  28.8 12.8 %all_to_all.5.heard_ref = f32[32,1,128]{2,1,0:T(1,128)S(1)} all-to-all(f32[32,1,128]{2,1,0:T(1,128)S(1)} %second.1), channel_id=1, replica_groups=mesh['sens'=8,'hour'=4] {'sens','hour'}, dimensions={0} | all-to-all | bytes 32768 | tf_op jit(solution)/shard_map/all_to_all | solution.py:354
  41.6 0.0 collective-permute-done.5.refs_3_
  41.6 1.4 %last.1 = (bf16[128,2048]{1,0:T(8,128)(2,1)}, f32[8,128]{1,0:T(8,128)}) custom-call(s32[1]{0:T(128)} %bitcast.me_ref.place_ref, s32[1]{0:T(128)} %bitcast.1.own_ref, f32[32,1,128]{2,1,0:T(1,128)S(1)} %all_to_all.5.heard_ref, s32[8,128]{1,0:T(8,128)S(1)} %get-tuple-element.38.zone_ref, f32[8,128]{1,0:T(8,128)S(1)} %get-tuple-element.39.area_ref, ...), custom_call_target="tpu_custom_call" | custom-call | tf_op jit(solution)/shard_map/last/pallas_call | solution.py:31
Async XLA Ops:
  1.6 21.6 %collective-permute-start = (bf16[168,512]{1,0:T(8,128)(2,1)S(1)}, bf16[168,512]{1,0:T(8,128)(2,1)S(1)}, u32[]{:S(2)}, u32[]{:S(2)}) collective-permute-start(bf16[168,512]{1,0:T(8,128)(2,1)S(1)} %get-tuple-element.23), channel_id=1, source_target_pairs={{0,3},{1,2},{2,1},{3,0},{4,7},{5,6},{6,5},{7,4},{8,11},{9,10},{10,... | collective-permute-start | bytes 516104 | tf_op jit(solution)/shard_map/ppermute | solution.py:37
  6.8 7.4 %collective-permute-start.1 = (bf16[16,128]{1,0:T(8,128)(2,1)S(1)}, bf16[16,128]{1,0:T(8,128)(2,1)S(1)}, u32[]{:S(2)}, u32[]{:S(2)}) collective-permute-start(bf16[16,128]{1,0:T(8,128)(2,1)S(1)} %get-tuple-element.25.refs_0_.refs_1_), channel_id=1, source_target_pairs={{0,2},{1,3},{2,0},{3,1},{4,6},{5,7},{6,4},{7,5},{8,10},{9,11},{10,... | collective-permute-start | bytes 12296 | tf_op jit(solution)/shard_map/ppermute | solution.py:37
  16.1 3.8 %collective-permute-start.2 = (bf16[32,128]{1,0:T(8,128)(2,1)S(1)}, bf16[32,128]{1,0:T(8,128)(2,1)S(1)}, u32[]{:S(2)}, u32[]{:S(2)}) collective-permute-start(bf16[32,128]{1,0:T(8,128)(2,1)S(1)} %get-tuple-element.27), channel_id=1, source_target_pairs={{0,1},{1,0},{2,3},{3,2},{4,5},{5,4},{6,7},{7,6},{8,9},{9,8},{10,11... | collective-permute-start | bytes 24584 | tf_op jit(solution)/shard_map/ppermute | solution.py:37
  16.2 12.0 %collective-permute-start.3 = (s16[136,512]{1,0:T(8,128)(2,1)S(1)}, s16[136,512]{1,0:T(8,128)(2,1)S(1)}, u32[]{:S(2)}, u32[]{:S(2)}) collective-permute-start(s16[136,512]{1,0:T(8,128)(2,1)S(1)} %get-tuple-element.34), channel_id=1, source_target_pairs={{0,2},{1,3},{2,0},{3,1},{4,6},{5,7},{6,4},{7,5},{8,10},{9,11},{10,... | collective-permute-start | bytes 417800 | tf_op jit(solution)/shard_map/ppermute | solution.py:37
  23.1 5.4 %collective-permute-start.4 = (s16[136,512]{1,0:T(8,128)(2,1)S(1)}, s16[136,512]{1,0:T(8,128)(2,1)S(1)}, u32[]{:S(2)}, u32[]{:S(2)}) collective-permute-start(s16[136,512]{1,0:T(8,128)(2,1)S(1)} %get-tuple-element.37), channel_id=1, source_target_pairs={{0,1},{1,0},{2,3},{3,2},{4,5},{5,4},{6,7},{7,6},{8,9},{9,8},{10,11... | collective-permute-start | bytes 417800 | tf_op jit(solution)/shard_map/ppermute | solution.py:37
  25.8 15.8 %collective-permute-start.5 = (s16[136,512]{1,0:T(8,128)(2,1)}, s16[136,512]{1,0:T(8,128)(2,1)S(1)}, u32[]{:S(2)}, u32[]{:S(2)}) collective-permute-start(s16[136,512]{1,0:T(8,128)(2,1)} %get-tuple-element.41), channel_id=1, source_target_pairs={{0,3},{1,2},{2,1},{3,0},{4,7},{5,6},{6,5},{7,4},{8,11},{9,10},{10,... | collective-permute-start | bytes 417800 | tf_op jit(solution)/shard_map/ppermute | solution.py:37

commit v3 on v1

--- a/solution.py
+++ b/solution.py
@@ -249,7 +249,7 @@
         in_specs=[HBM, HBM],
         scratch_shapes=[pltpu.VMEM((kbins, rows), jnp.int32), pltpu.VMEM((kbins, rows), bf16), dma(2)],
     )(sun_bins.T, sun_rad.T)
-    heads = exchange(packed, "hour", 3)
+    heads = exchange(packed, "hour", 2)
 
     tiles = (windows // LANES, LANES)
     message = pl.cdiv(5 * zones, LANES) * LANES
@@ -280,10 +280,10 @@
 
     codes = [None] * groups
     code, late, both = sun([(1, 0)], sun_coef, True, packed, heads)
-    codes[3] = exchange(code, "hour", 3)
+    codes[2] = exchange(code, "hour", 2)
     heads = exchange(both, "hour", 1)
     (code,) = sun([(0, HEAD)], late, False, heads)
-    codes[2] = exchange(code, "hour", 2)
+    codes[3] = exchange(code, "hour", 3)
     code, codes[0] = sun([(0, 0), (1, 0)], late, False, heads, packed)
     codes[1] = exchange(code, "hour", 1)
 
@@ -300,7 +300,7 @@
             dma(4),
         ],
     )(codes[0], sky.T, sky_open, sky_closed, target)
-    first, second = [3, 2, 0], [1]
+    first, second = [2, 3, 0], [1]
     first_sums = call(
         first_kernel(first),
         "first",

time: 40.6 us -> 38.7 us (0.953)
  starting transfers between devices: 13.6 us -> 11.5 us
  waiting for transfers between devices: 2.63 us -> 3.12 us
    ppermute x5, starting transfers between devices: 13.6 us -> 11.5 us  [exchange(): lax.ppermute(x, axis, [(i, i ^ mask) for i in range(lax.axis_size(axis))])]
    ppermute x5, waiting for transfers between devices: 2.63 us -> 3.12 us  [exchange(): lax.ppermute(x, axis, [(i, i ^ mask) for i in range(lax.axis_size(axis))])]
  transfers between devices with their start and end apart: 5 -> 5, of which waited for: 3 -> 3; matrix products, arithmetic and copies ran while one was open for 0% -> 0% of each run, Pallas kernels for 19% -> 20%
where the time goes in v3:
time: 38.7 us; the launch traced here: 38.5 us
  Pallas kernels  12.1 us (31%)
  starting transfers between devices  11.5 us (30%)
  blocking collectives  11.1 us (29%)
  waiting for transfers between devices  3.12 us (8%)
  between operations  0.71 us (2%)
    pallas_call x9, Pallas kernels, call(): run(*[pltpu.with_memory_space_constraint(x, pltpu.HBM) if s is HBM else x...  12.1 us
    ppermute x5, starting transfers between devices, exchange(): lax.ppermute(x, axis, [(i, i ^ mask) for i in range(lax.axis_size(axis))])  11.5 us
    all_to_all x1, blocking collectives, local(): heard = lax.all_to_all(sent, ('sens', 'hour'), 0, 0)  11.1 us
    ppermute x5, waiting for transfers between devices, exchange(): lax.ppermute(x, axis, [(i, i ^ mask) for i in range(lax.axis_size(axis))])  3.12 us
  transfers between devices with their start and end apart: 5, of which 3 were waited for; matrix products, arithmetic and copies ran while one was open for 0% of the time, Pallas kernels for 20%

profile of v3, /device:TPU:0, one launch (start us, length us, event | category | flops | bytes accessed | tf_op | source)
XLA Modules:
  0.0 38.5 jit_solution(18324108884020091235)
XLA Ops:
  0.6 0.7 %pack.1.refs_0_.refs_1_ = bf16[16,128]{1,0:T(8,128)(2,1)S(1)} custom-call(s32[4,128]{1,0:T(4,128)} %bitcast.13, bf16[4,128]{1,0:T(4,128)(2,1)} %bitcast.14), custom_call_target="tpu_custom_call" | custom-call | tf_op jit(solution)/shard_map/pack/pallas_call | solution.py:31
  1.4 4.1 %collective-permute-start = (bf16[16,128]{1,0:T(8,128)(2,1)S(1)}, bf16[16,128]{1,0:T(8,128)(2,1)S(1)}, u32[]{:S(2)}, u32[]{:S(2)}) collective-permute-start(bf16[16,128]{1,0:T(8,128)(2,1)S(1)} %pack.1.refs_0_.refs_1_), channel_id=1, source_target_pairs={{0,2},{1,3},{2,0},{3,1},{4,6},{5,7},{6,4},{7,5},{8,10},{9,11},{10,... | collective-permute-start | bytes 12296 | tf_op jit(solution)/shard_map/ppermute | solution.py:37
  5.5 2.0 %fetch.1 = (bf16[3072,512]{1,0:T(8,128)(2,1)S(1)}, f32[1,128]{1,0:T(1,128)S(1)}, s32[8,128]{1,0:T(8,128)S(1)}, f32[8,128]{1,0:T(8,128)S(1)}, f32[8,128]{1,0:T(8,128)S(1)}) custom-call(bf16[5165,512]{1,0:T(8,128)(2,1)} %rest_in.1, s32[8,128]{1,0:T(8,128)} %bitcast.10, f32[8,128]{1,0:T(8,128)} %bitcast.11, f32[8,128]{1,0:T(8,128)} %bitcast.12), custom_call_target="tpu_custom_call" | custom-call | tf_op jit(solution)/shard_map/fetch/pallas_call | solution.py:31
  7.4 0.0 collective-permute-done.refs_1_
  7.5 2.0 %sun.3 = (s16[136,512]{1,0:T(8,128)(2,1)S(1)}, bf16[2093,512]{1,0:T(8,128)(2,1)S(1)}, bf16[32,128]{1,0:T(8,128)(2,1)S(1)}) custom-call(bf16[3072,512]{1,0:T(8,128)(2,1)S(1)} %get-tuple-element.17.first_ref, bf16[5165,512]{1,0:T(8,128)(2,1)} %rest_in.1, bf16[16,128]{1,0:T(8,128)(2,1)S(1)} %pack.1.refs_0_.refs_1_, bf16[16,128]{1,0:T(8,128)(2,1)S(1)} %collective-permute-done.refs_1_), custom_call_target="tpu_custom_call" | custom-call | tf_op jit(solution)/shard_map/sun/pallas_call | solution.py:31
  9.5 1.6 %collective-permute-start.1 = (bf16[32,128]{1,0:T(8,128)(2,1)S(1)}, bf16[32,128]{1,0:T(8,128)(2,1)S(1)}, u32[]{:S(2)}, u32[]{:S(2)}) collective-permute-start(bf16[32,128]{1,0:T(8,128)(2,1)S(1)} %get-tuple-element.19), channel_id=1, source_target_pairs={{0,1},{1,0},{2,3},{3,2},{4,5},{5,4},{6,7},{7,6},{8,9},{9,8},{10,11... | collective-permute-start | bytes 24584 | tf_op jit(solution)/shard_map/ppermute | solution.py:37
  11.1 2.5 %collective-permute-start.2 = (s16[136,512]{1,0:T(8,128)(2,1)S(1)}, s16[136,512]{1,0:T(8,128)(2,1)S(1)}, u32[]{:S(2)}, u32[]{:S(2)}) collective-permute-start(s16[136,512]{1,0:T(8,128)(2,1)S(1)} %get-tuple-element.24), channel_id=1, source_target_pairs={{0,2},{1,3},{2,0},{3,1},{4,6},{5,7},{6,4},{7,5},{8,10},{9,11},{10,... | collective-permute-start | bytes 417800 | tf_op jit(solution)/shard_map/ppermute | solution.py:37
  13.6 0.0 collective-permute-done.1.refs_0_
  13.6 1.3 %sun.5 = s16[136,512]{1,0:T(8,128)(2,1)S(1)} custom-call(bf16[3072,512]{1,0:T(8,128)(2,1)S(1)} %get-tuple-element.17.first_ref, bf16[2093,512]{1,0:T(8,128)(2,1)S(1)} %get-tuple-element.18.rest_in, bf16[32,128]{1,0:T(8,128)(2,1)S(1)} %collective-permute-done.1.refs_0_), custom_call_target="tpu_custom_call" | custom-call | tf_op jit(solution)/shard_map/sun/pallas_call | solution.py:31
  14.9 3.1 %collective-permute-start.3 = (s16[136,512]{1,0:T(8,128)(2,1)S(1)}, s16[136,512]{1,0:T(8,128)(2,1)S(1)}, u32[]{:S(2)}, u32[]{:S(2)}) collective-permute-start(s16[136,512]{1,0:T(8,128)(2,1)S(1)} %sun.5), channel_id=1, source_target_pairs={{0,3},{1,2},{2,1},{3,0},{4,7},{5,6},{6,5},{7,4},{8,11},{9,10},{10,... | collective-permute-start | bytes 417800 | tf_op jit(solution)/shard_map/ppermute | solution.py:37
  18.1 2.2 %sun.4 = (s16[136,512]{1,0:T(8,128)(2,1)S(1)}, s16[136,512]{1,0:T(8,128)(2,1)S(1)}) custom-call(bf16[3072,512]{1,0:T(8,128)(2,1)S(1)} %get-tuple-element.17.first_ref, bf16[2093,512]{1,0:T(8,128)(2,1)S(1)} %get-tuple-element.18.rest_in, bf16[32,128]{1,0:T(8,128)(2,1)S(1)} %collective-permute-done.1.refs_0_, bf16[16,128]{1,0:T(8,128)(2,1)S(1)} %pack.1.refs_0_.refs_1_), custom_call_target="tpu_custom_call" | custom-call | tf_op jit(solution)/shard_map/sun/pallas_call | solution.py:31
  20.3 0.1 collective-permute-start.4
  20.4 1.8 %base.1 = (f32[128,2048]{1,0:T(8,128)S(1)}, f32[128,2048]{1,0:T(8,128)S(1)}, bf16[128,2048]{1,0:T(8,128)(2,1)S(1)}) custom-call(s16[136,512]{1,0:T(8,128)(2,1)S(1)} %get-tuple-element.20.token.refs_2_.refs_0_, bf16[146,128]{1,0:T(8,128)(2,1)} %bitcast.9, bf16[146,2048]{1,0:T(8,128)(2,1)} %open_hbm.1, bf16[146,2048]{1,0:T(8,128)(2,1)} %closed_hbm.1, ...), custom_call_target="tpu_custom_call" | custom-call | tf_op jit(solution)/shard_map/base/pallas_call | solution.py:31
  22.2 0.3 collective-permute-done.2.refs_0_.refs_2_
  22.5 0.7 %collective-permute-done.3.refs_1_.refs_3_ = s16[136,512]{1,0:T(8,128)(2,1)S(1)} collective-permute-done((s16[136,512]{1,0:T(8,128)(2,1)S(1)}, s16[136,512]{1,0:T(8,128)(2,1)S(1)}, u32[]{:S(2)}, u32[]{:S(2)}) %collective-permute-start.3) | collective-permute-done | bytes 139296 | tf_op jit(solution)/shard_map/ppermute | solution.py:37
  23.2 0.4 first.1.first_ref
  23.5 2.1 %collective-permute-done.4.refs_0_.refs_1_ = s16[136,512]{1,0:T(8,128)(2,1)S(1)} collective-permute-done((s16[136,512]{1,0:T(8,128)(2,1)S(1)}, s16[136,512]{1,0:T(8,128)(2,1)S(1)}, u32[]{:S(2)}, u32[]{:S(2)}) %collective-permute-start.4) | collective-permute-done | bytes 139296 | tf_op jit(solution)/shard_map/ppermute | solution.py:37
  25.7 0.3 second.1
  26.0 11.1 %all_to_all.5.heard_ref = f32[32,1,128]{2,1,0:T(1,128)S(1)} all-to-all(f32[32,1,128]{2,1,0:T(1,128)S(1)} %second.1), channel_id=1, replica_groups=mesh['sens'=8,'hour'=4] {'sens','hour'}, dimensions={0} | all-to-all | bytes 32768 | tf_op jit(solution)/shard_map/all_to_all | solution.py:316
  37.0 1.4 %last.1 = (bf16[128,2048]{1,0:T(8,128)(2,1)}, f32[8,128]{1,0:T(8,128)}) custom-call(s32[1]{0:T(128)} %bitcast.me_ref.place_ref, s32[1]{0:T(128)} %bitcast.1.own_ref, f32[32,1,128]{2,1,0:T(1,128)S(1)} %all_to_all.5.heard_ref, s32[8,128]{1,0:T(8,128)S(1)} %get-tuple-element.27.zone_ref, f32[8,128]{1,0:T(8,128)S(1)} %get-tuple-element.28.area_ref, ...), custom_call_target="tpu_custom_call" | custom-call | tf_op jit(solution)/shard_map/last/pallas_call | solution.py:31
Async XLA Ops:
  1.4 6.1 %collective-permute-start = (bf16[16,128]{1,0:T(8,128)(2,1)S(1)}, bf16[16,128]{1,0:T(8,128)(2,1)S(1)}, u32[]{:S(2)}, u32[]{:S(2)}) collective-permute-start(bf16[16,128]{1,0:T(8,128)(2,1)S(1)} %pack.1.refs_0_.refs_1_), channel_id=1, source_target_pairs={{0,2},{1,3},{2,0},{3,1},{4,6},{5,7},{6,4},{7,5},{8,10},{9,11},{10,... | collective-permute-start | bytes 12296 | tf_op jit(solution)/shard_map/ppermute | solution.py:37
  9.5 4.2 %collective-permute-start.1 = (bf16[32,128]{1,0:T(8,128)(2,1)S(1)}, bf16[32,128]{1,0:T(8,128)(2,1)S(1)}, u32[]{:S(2)}, u32[]{:S(2)}) collective-permute-start(bf16[32,128]{1,0:T(8,128)(2,1)S(1)} %get-tuple-element.19), channel_id=1, source_target_pairs={{0,1},{1,0},{2,3},{3,2},{4,5},{5,4},{6,7},{7,6},{8,9},{9,8},{10,11... | collective-permute-start | bytes 24584 | tf_op jit(solution)/shard_map/ppermute | solution.py:37
  11.1 11.4 %collective-permute-start.2 = (s16[136,512]{1,0:T(8,128)(2,1)S(1)}, s16[136,512]{1,0:T(8,128)(2,1)S(1)}, u32[]{:S(2)}, u32[]{:S(2)}) collective-permute-start(s16[136,512]{1,0:T(8,128)(2,1)S(1)} %get-tuple-element.24), channel_id=1, source_target_pairs={{0,2},{1,3},{2,0},{3,1},{4,6},{5,7},{6,4},{7,5},{8,10},{9,11},{10,... | collective-permute-start | bytes 417800 | tf_op jit(solution)/shard_map/ppermute | solution.py:37
  14.9 8.2 %collective-permute-start.3 = (s16[136,512]{1,0:T(8,128)(2,1)S(1)}, s16[136,512]{1,0:T(8,128)(2,1)S(1)}, u32[]{:S(2)}, u32[]{:S(2)}) collective-permute-start(s16[136,512]{1,0:T(8,128)(2,1)S(1)} %sun.5), channel_id=1, source_target_pairs={{0,3},{1,2},{2,1},{3,0},{4,7},{5,6},{6,5},{7,4},{8,11},{9,10},{10,... | collective-permute-start | bytes 417800 | tf_op jit(solution)/shard_map/ppermute | solution.py:37
  20.3 5.4 %collective-permute-start.4 = (s16[136,512]{1,0:T(8,128)(2,1)S(1)}, s16[136,512]{1,0:T(8,128)(2,1)S(1)}, u32[]{:S(2)}, u32[]{:S(2)}) collective-permute-start(s16[136,512]{1,0:T(8,128)(2,1)S(1)} %get-tuple-element.26), channel_id=1, source_target_pairs={{0,1},{1,0},{2,3},{3,2},{4,5},{5,4},{6,7},{7,6},{8,9},{9,8},{10,11... | collective-permute-start | bytes 417800 | tf_op jit(solution)/shard_map/ppermute | solution.py:37
